TPU v7x, 32 devices: a whole 2x2x4 slice. The times are simulated.
32 devices in a mesh: section: 4 (over z), seq: 8 (over y, x, core).
Axes of the slice: x: 2, y: 2, z: 4, core: 2. Of those that a mesh axis runs over, the one named last changes fastest.
Arguments:
- section_input: bfloat16 [4, 8192, 1024], P('section', 'seq'), may hold values from -6 to 6
- stashed_input: bfloat16 [4, 8192, 1024], P('section', 'seq'), may hold values from -6 to 6
- output_grad: bfloat16 [4, 8192, 1024], P('section', 'seq'), may hold values from -6 to 6
- gain_mixer: float32 [4, 1024], P('section'), may hold values from 0.1 to 1.9
- gain_channel: float32 [4, 1024], P('section'), may hold values from 0.1 to 1.9
- factor_first: bfloat16 [4, 64, 128, 128], P('section', 'seq'), may hold values from -0.5 to 0.5
- factor_second: bfloat16 [4, 128, 64, 64], P('section', 'seq'), may hold values from -0.75 to 0.75
- spectrum: bfloat16 [4, 64, 128, 1024], P('section', None, 'seq'), may hold values from -6 to 6
- factor_third: bfloat16 [4, 128, 64, 64], P('section', 'seq'), may hold values from -0.75 to 0.75
- factor_fourth: bfloat16 [4, 64, 128, 128], P('section', 'seq'), may hold values from -0.5 to 0.5
- mixer_gate: bfloat16 [4, 1024, 256], P('section'), may hold values from -0.375 to 0.375
- channel_up: bfloat16 [4, 1024, 512], P('section'), may hold values from -0.375 to 0.375
- channel_gate: bfloat16 [4, 1024, 512], P('section'), may hold values from -0.375 to 0.375
- channel_down: bfloat16 [4, 2048, 256], P('section'), may hold values from -0.25 to 0.25
Outputs:
- next_input: bfloat16 [4, 8192, 1024], P('section', 'seq')
- upstream_grad: bfloat16 [4, 8192, 1024], P('section', 'seq')
- spectrum_grad: bfloat16 [4, 64, 128, 1024], P('section', None, 'seq')
- mixer_gate_grad: bfloat16 [4, 1024, 256], P('section', 'seq')
- channel_up_grad: bfloat16 [4, 1024, 512], P('section', 'seq')
- channel_gate_grad: bfloat16 [4, 1024, 512], P('section', 'seq')
- channel_down_grad: bfloat16 [4, 2048, 256], P('section', 'seq')
All inputs are finite; a program needn't handle non-finite values.
Results may differ from a plain program's by a relative error of at most 0.017.
Values may be sent and summed in bfloat16 or wider, within the bound.
A program may use at most 128 MiB of HBM per device.

v0:
```python
import math

import jax
import jax.numpy as jnp
from jax import lax
from jax.sharding import PartitionSpec as P

NB = 4
NI = 64
NJ = 128


epsilon = 1e-06


def from_behind(array, axis, by):
    length = lax.axis_size(axis)
    pairs = [(i, i + by) for i in range(length) if 0 <= i + by < length]
    return lax.ppermute(array, axis, pairs)


def bround(value):
    return lax.optimization_barrier(value.astype(jnp.bfloat16))


def rms_scale(value_array):
    return lax.rsqrt(jnp.mean(value_array * value_array, axis=-1, keepdims=True) + epsilon)


def norm_back(value_array, scale, gain, incoming_gradient):
    scaled = gain * incoming_gradient
    return scale * scaled - value_array * (scale * scale * scale) * jnp.mean(
        scaled * value_array, axis=-1, keepdims=True
    )


def block_apply(value_array, weight, block_list):
    item_count = value_array.shape[0]
    reshaped_array = weight.reshape(block_list, weight.shape[0] // block_list, weight.shape[1])
    final_output = jnp.einsum(
        "ynq,nqd->ynd",
        value_array.reshape(item_count, block_list, -1),
        reshaped_array,
        preferred_element_type=jnp.float32,
    )
    return final_output.reshape(item_count, -1)


def block_back(incoming_gradient, weight, block_list):
    item_count = incoming_gradient.shape[0]
    reshaped_array = weight.reshape(block_list, weight.shape[0] // block_list, weight.shape[1])
    final_output = jnp.einsum(
        "eaq,awq->eaw",
        incoming_gradient.reshape(item_count, block_list, -1),
        reshaped_array,
        preferred_element_type=jnp.float32,
    )
    return final_output.reshape(item_count, -1)


def block_grad(value_array, incoming_gradient, block_list):
    item_count = value_array.shape[0]
    final_output = jnp.einsum(
        "wli,wld->lid",
        value_array.reshape(item_count, block_list, -1),
        incoming_gradient.reshape(item_count, block_list, -1),
        preferred_element_type=jnp.float32,
    )
    return final_output.reshape(-1, final_output.shape[2])


def shuffle(value_array, block_list):
    item_count = value_array.shape[0]
    return (
        value_array.reshape(item_count, block_list, block_list, -1)
        .transpose(0, 2, 1, 3)
        .reshape(item_count, -1)
    )


def mixer_front(wide, gain, first, row_count, col_count):
    scale = rms_scale(wide)
    normed = (wide * scale * gain).astype(jnp.bfloat16)
    folded = jnp.einsum(
        "iqj,ijc->iqc",
        first,
        normed.reshape(row_count, col_count, -1),
        preferred_element_type=jnp.float32,
    )
    return (scale, normed, folded.astype(jnp.bfloat16))


def mixer_middle(received, second, kernel_here, third):
    mixed = jnp.einsum("jpi,ijc->pjc", second, received, preferred_element_type=jnp.float32)
    filtered = (mixed * kernel_here).astype(jnp.bfloat16)
    returned = jnp.einsum("jpi,ijc->pjc", third, filtered, preferred_element_type=jnp.float32)
    return (mixed, returned.astype(jnp.bfloat16))


def layer_tail(
    wide,
    normed,
    collected,
    fourth_factor,
    gain,
    mixing_weight,
    up_weight,
    activation_weight,
    down_weight,
    block_list,
):
    item_count = wide.shape[0]
    back_mixed = jnp.einsum(
        "iqj,ijc->iqc", fourth_factor, collected, preferred_element_type=jnp.float32
    ).reshape(item_count, -1)
    gating = block_apply(normed, mixing_weight, block_list)
    middle = bround(wide + back_mixed * gating)
    middle_wide = middle.astype(jnp.float32)
    scale_two = rms_scale(middle_wide)
    normed_two = (middle_wide * scale_two * gain).astype(jnp.bfloat16)
    lifted = block_apply(normed_two, up_weight, block_list)
    gated = block_apply(normed_two, activation_weight, block_list)
    hidden = (jax.nn.silu(gated) * lifted).astype(jnp.bfloat16)
    shuffled = shuffle(hidden, block_list)
    output = (middle_wide + block_apply(shuffled, down_weight, block_list)).astype(jnp.bfloat16)
    return (
        output,
        (back_mixed, gating, middle_wide, scale_two, normed_two, lifted, gated, shuffled),
    )


def shards(
    section_input,
    stashed_input,
    output_grad,
    gain_mixer,
    gain_channel,
    factor_first,
    factor_second,
    spectrum,
    factor_third,
    factor_fourth,
    mixer_gate,
    channel_up,
    channel_gate,
    channel_down,
):
    first = factor_first[0]
    second = factor_second[0]
    kernel_here = spectrum[0]
    third = factor_third[0]
    fourth_factor = factor_fourth[0]
    mixing_weight = mixer_gate[0]
    up_weight = channel_up[0]
    activation_weight = channel_gate[0]
    down_weight = channel_down[0]
    gain_one = gain_mixer[0]
    second_gain = gain_channel[0]
    block_list = NB
    row_count = first.shape[0]
    col_count = first.shape[1]
    grad_factor = 1.0 / math.sqrt(NI * NJ)
    expanded_forward = section_input[0].astype(jnp.float32)
    expanded_backward = stashed_input[0].astype(jnp.float32)
    scale_fwd, normalized_forward, folded_fwd = mixer_front(
        expanded_forward, gain_one, first, row_count, col_count
    )
    scale_back, normalized_backward, folded_back = mixer_front(
        expanded_backward, gain_one, first, row_count, col_count
    )
    recv_fwd, recv_back = (
        lax.all_to_all(folded_fwd, "seq", split_axis=1, concat_axis=0, tiled=True),
        lax.all_to_all(folded_back, "seq", split_axis=1, concat_axis=0, tiled=True),
    )
    mixed_fwd, returned_fwd = mixer_middle(recv_fwd, second, kernel_here, third)
    mixed_back, returned_back = mixer_middle(recv_back, second, kernel_here, third)
    gathered_forward, gathered_backward = (
        lax.all_to_all(returned_fwd, "seq", split_axis=0, concat_axis=1, tiled=True),
        lax.all_to_all(returned_back, "seq", split_axis=0, concat_axis=1, tiled=True),
    )
    output_fwd, unused = layer_tail(
        expanded_forward,
        normalized_forward,
        gathered_forward,
        fourth_factor,
        second_gain,
        mixing_weight,
        up_weight,
        activation_weight,
        down_weight,
        block_list,
    )
    next_input = from_behind(output_fwd[None], "section", 1)
    output_back, saved = layer_tail(
        expanded_backward,
        normalized_backward,
        gathered_backward,
        fourth_factor,
        second_gain,
        mixing_weight,
        up_weight,
        activation_weight,
        down_weight,
        block_list,
    )
    back_mixed, gating, middle_wide, scale_two, normed_two, lifted, gated, shuffled = saved
    incoming_gradient = output_grad[0]
    up_wide = incoming_gradient.astype(jnp.float32)
    d_shuffled = bround(block_back(incoming_gradient, down_weight, block_list))
    d_hidden = shuffle(d_shuffled, block_list).astype(jnp.float32)
    sigma = jax.nn.sigmoid(gated)
    d_lift = (d_hidden * gated * sigma).astype(jnp.bfloat16)
    d_gated = (d_hidden * lifted * sigma * (1.0 + gated * (1.0 - sigma))).astype(jnp.bfloat16)
    d_norm_two = block_back(d_lift, up_weight, block_list) + block_back(
        d_gated, activation_weight, block_list
    )
    d_middle = bround(up_wide + norm_back(middle_wide, scale_two, second_gain, d_norm_two))
    d_mid_wide = d_middle.astype(jnp.float32)
    d_back = (d_mid_wide * gating).astype(jnp.bfloat16)
    d_gating = (d_mid_wide * back_mixed).astype(jnp.bfloat16)
    d_returned = jnp.einsum(
        "iqj,iqc->ijc",
        fourth_factor,
        d_back.reshape(row_count, col_count, -1),
        preferred_element_type=jnp.float32,
    ).astype(jnp.bfloat16)
    d_recv = lax.all_to_all(d_returned, "seq", split_axis=1, concat_axis=0, tiled=True)
    d_filtered = jnp.einsum("jpi,pjc->ijc", third, d_recv, preferred_element_type=jnp.float32)
    kernel_grad = (d_filtered * mixed_back).astype(jnp.bfloat16)
    d_mixed = (d_filtered * kernel_here).astype(jnp.bfloat16)
    d_folded = jnp.einsum(
        "jpi,pjc->ijc", second, d_mixed, preferred_element_type=jnp.float32
    ).astype(jnp.bfloat16)
    d_rows = lax.all_to_all(d_folded, "seq", split_axis=0, concat_axis=1, tiled=True)
    item_count = expanded_backward.shape[0]
    d_normed = jnp.einsum(
        "iqj,iqc->ijc", first, d_rows, preferred_element_type=jnp.float32
    ).reshape(item_count, -1)
    d_normed = d_normed + block_back(d_gating, mixing_weight, block_list)
    d_input = (d_mid_wide + norm_back(expanded_backward, scale_back, gain_one, d_normed)).astype(
        jnp.bfloat16
    )
    upstream_grad = from_behind(d_input[None], "section", -1)
    term_mix = block_grad(normalized_backward, d_gating, block_list) * grad_factor
    term_up = block_grad(normed_two, d_lift, block_list) * grad_factor
    term_act = block_grad(normed_two, d_gated, block_list) * grad_factor
    term_down = block_grad(shuffled, incoming_gradient, block_list) * grad_factor
    part_mix, part_up, part_act, part_down = (
        lax.psum_scatter(
            term_mix.astype(jnp.bfloat16), "seq", scatter_dimension=0, tiled=True
        ).astype(jnp.float32),
        lax.psum_scatter(
            term_up.astype(jnp.bfloat16), "seq", scatter_dimension=0, tiled=True
        ).astype(jnp.float32),
        lax.psum_scatter(
            term_act.astype(jnp.bfloat16), "seq", scatter_dimension=0, tiled=True
        ).astype(jnp.float32),
        lax.psum_scatter(
            term_down.astype(jnp.bfloat16), "seq", scatter_dimension=0, tiled=True
        ).astype(jnp.float32),
    )
    return (
        next_input,
        upstream_grad,
        kernel_grad[None],
        part_mix.astype(jnp.bfloat16)[None],
        part_up.astype(jnp.bfloat16)[None],
        part_act.astype(jnp.bfloat16)[None],
        part_down.astype(jnp.bfloat16)[None],
    )


def solution(mesh):
    in_specs = (
        P("section", "seq", None),
        P("section", "seq", None),
        P("section", "seq", None),
        P("section", None),
        P("section", None),
        P("section", "seq", None, None),
        P("section", "seq", None, None),
        P("section", None, "seq", None),
        P("section", "seq", None, None),
        P("section", "seq", None, None),
        P("section", None, None),
        P("section", None, None),
        P("section", None, None),
        P("section", None, None),
    )
    out_specs = (
        P("section", "seq", None),
        P("section", "seq", None),
        P("section", None, "seq", None),
        P("section", "seq", None),
        P("section", "seq", None),
        P("section", "seq", None),
        P("section", "seq", None),
    )
    return jax.shard_map(shards, mesh=mesh, in_specs=in_specs, out_specs=out_specs, check_vma=False)
```

profile of v0, /device:TPU:0, one launch (start us, length us, event | category | flops | bytes accessed | tf_op | source)
XLA Modules:
  0.0 409.9 jit_solution(16610215583898529965)
XLA Ops:
  11.5 2.4 convert_bitcast_fusion.5
  13.9 4.3 %copy.122 = bf16[8,128,1024]{2,0,1:T(8,128)(2,1)} copy(bf16[8,128,1024]{1,2,0:T(8,128)(2,1)} %convert_bitcast_fusion.5) | data formatting | bytes 4194304 | tf_op jit(solution)/shard_map/convert_element_type | solution.py:90
  18.2 5.2 %all-to-all-start = ((bf16[8,128,1024]{2,0,1:T(8,128)(2,1)}), bf16[8,128,1024]{2,0,1:T(8,128)(2,1)}, u32[]{:S(2)}, u32[]{:S(2)}) async-start(bf16[8,128,1024]{2,0,1:T(8,128)(2,1)} %copy.122), calls=%async_computation | async-start | bytes 4194304 | tf_op jit(solution)/shard_map/all_to_all | solution.py:172
  25.9 2.4 convert_bitcast_fusion.3
  28.3 4.1 %copy.141 = bf16[8,128,1024]{2,0,1:T(8,128)(2,1)} copy(bf16[8,128,1024]{1,2,0:T(8,128)(2,1)} %convert_bitcast_fusion.3) | data formatting | bytes 4194304 | tf_op jit(solution)/shard_map/convert_element_type | solution.py:90
  32.4 17.7 %all-to-all-done = bf16[8,128,1024]{2,0,1:T(8,128)(2,1)} async-done(((bf16[8,128,1024]{2,0,1:T(8,128)(2,1)}), bf16[8,128,1024]{2,0,1:T(8,128)(2,1)}, u32[]{:S(2)}, u32[]{:S(2)}) %all-to-all-start) | async-done | bytes 2097184 | tf_op jit(solution)/shard_map/all_to_all | solution.py:172
  50.1 4.6 %all-to-all-start.2 = ((bf16[8,128,1024]{2,0,1:T(8,128)(2,1)}), bf16[8,128,1024]{2,0,1:T(8,128)(2,1)}, u32[]{:S(2)}, u32[]{:S(2)}) async-start(bf16[8,128,1024]{2,0,1:T(8,128)(2,1)} %copy.141), calls=%async_computation.2 | async-start | bytes 4194304 | tf_op jit(solution)/shard_map/all_to_all | solution.py:173
  54.7 4.1 %copy.124 = bf16[8,8,16,1024]{3,2,1,0:T(8,128)(2,1)} copy(bf16[8,8,16,1024]{3,1,2,0:T(8,128)(2,1)} %bitcast.8) | data formatting | bytes 4194304 | tf_op jit(solution)/shard_map/all_to_all | solution.py:172
  58.8 9.3 %convert_bitcast_fusion.4 = bf16[64,16,1024]{2,0,1:T(8,128)(2,1)} fusion(bf16[64,16,1024]{2,1,0:T(8,128)(2,1)} %bitcast.345, bf16[1,64,16,1024]{3,2,1,0:T(8,128)(2,1)} %param.21, bf16[1,16,64,64]{3,2,1,0:T(8,128)(2,1)S(1)} %copy-done.39, bf16[1,16,64,64]{3,2,1,0:T(8,128)(2,1)} %param.20), kind=kOutput, calls=%fused_computation.110 | convolution fusion | flops 272629760 | bytes 6553600 | tf_op jit(solution)/shard_map/jpi,ijc->pjc/dot_general | solution.py:96
  68.1 4.1 copy.127
  72.1 9.2 %all-to-all-done.2 = bf16[8,128,1024]{2,0,1:T(8,128)(2,1)} async-done(((bf16[8,128,1024]{2,0,1:T(8,128)(2,1)}), bf16[8,128,1024]{2,0,1:T(8,128)(2,1)}, u32[]{:S(2)}, u32[]{:S(2)}) %all-to-all-start.2) | async-done | bytes 2097184 | tf_op jit(solution)/shard_map/all_to_all | solution.py:173
  81.3 4.6 %all-to-all-start.1 = ((bf16[64,16,1024]{2,1,0:T(8,128)(2,1)}), bf16[64,16,1024]{2,1,0:T(8,128)(2,1)}, u32[]{:S(2)}, u32[]{:S(2)}) async-start(bf16[64,16,1024]{2,1,0:T(8,128)(2,1)} %copy.127), calls=%async_computation.1 | async-start | bytes 4194304 | tf_op jit(solution)/shard_map/all_to_all | solution.py:178
  86.0 4.2 %copy.200 = f32[1,1024,1024]{1,2,0:T(8,128)} copy(bf16[1,1024,1024]{2,1,0:T(8,128)(2,1)} %param.14) | data formatting | bytes 6291456 | tf_op jit(solution)/shard_map/convert_element_type | solution.py:163
  90.1 3.0 copy.202
  94.3 4.5 %reshape_squeeze.27 = bf16[1024,4,256]{2,1,0:T(4,128)(2,1)} reshape(bf16[1,1024,1024]{2,1,0:T(8,128)(2,1)} %param.16) | data formatting | bytes 4194304 | tf_op jit(solution)/shard_map/reshape;squeeze | solution.py:54
  98.8 5.3 %fusion.44 = f32[4,1024,256]{1,2,0:T(8,128)} fusion(bf16[4,256,256]{2,1,0:T(8,128)(2,1)} %bitcast.350, f32[1024,4,256]{0,2,1:T(8,128)} %bitcast.329, f32[4,256]{1,0:T(4,128)S(1)} %mul.298, f32[1024]{0:T(1024)S(1)} %get-tuple-element.40), kind=kOutput, calls=%fused_computation.77 | convolution fusion | flops 540016640 | bytes 8921088 | tf_op jit(solution)/shard_map/ynq,nqd->ynd/dot_general | solution.py:40
  104.2 2.4 fusion.65
  106.6 2.8 convert_bitcast_fusion.2
  109.5 2.5 copy.144
  112.6 4.4 %all-to-all-start.3 = ((bf16[64,16,1024]{2,1,0:T(8,128)(2,1)}), bf16[64,16,1024]{2,1,0:T(8,128)(2,1)}, u32[]{:S(2)}, u32[]{:S(2)}) async-start(bf16[64,16,1024]{2,1,0:T(8,128)(2,1)} %copy.144), calls=%async_computation.3 | async-start | bytes 4194304 | tf_op jit(solution)/shard_map/all_to_all | solution.py:179
  117.1 3.2 convolution_convert_fusion
  120.3 4.3 %copy.151 = f32[1024,4,4,128]{0,3,1,2:T(8,128)} copy(bf16[1024,4,4,128]{0,3,2,1:T(8,128)(2,1)S(1)} %bitcast.326) | data formatting | bytes 12582912 | tf_op jit(solution)/shard_map/convert_element_type | solution.py:210
  124.6 5.8 %copy.132 = f32[1024,1024]{1,0:T(8,128)} copy(f32[1024,1024]{0,1:T(8,128)} %bitcast.331) | data formatting | bytes 8388608 | tf_op jit(solution)/shard_map/reshape | solution.py:46
  130.4 5.3 %fusion.99 = f32[4,1024,256]{1,2,0:T(8,128)} fusion(bf16[4,256,256]{2,1,0:T(8,128)(2,1)} %bitcast.351, f32[1024,4,256]{0,2,1:T(8,128)} %bitcast.327, f32[1024]{0:T(1024)S(1)} %get-tuple-element.34, f32[4,256]{1,0:T(4,128)S(1)} %mul.298), kind=kOutput, calls=%fused_computation.127 | convolution fusion | flops 540016640 | bytes 8921088 | tf_op jit(solution)/shard_map/ynq,nqd->ynd/dot_general | solution.py:40
  135.7 5.4 %copy.149 = f32[1024,1024]{1,0:T(8,128)} copy(f32[1024,1024]{0,1:T(8,128)} %bitcast.332) | data formatting | bytes 8388608 | tf_op jit(solution)/shard_map/reshape | solution.py:46
  158.3 4.0 copy.205
  162.3 3.1 fusion.119
  165.5 13.3 %fusion.2 = (bf16[1024,4,512]{0,2,1:T(8,128)(2,1)S(1)}, bf16[1024,4,512]{0,2,1:T(8,128)(2,1)}, f32[4,1024,512]{1,2,0:T(8,128)}) fusion(f32[1024,4,4,128]{0,3,1,2:T(8,128)} %copy.151, f32[4,1024,512]{1,2,0:T(8,128)S(1)} %fusion.119, bf16[1024,4,256]{0,2,1:T(8,128)(2,1)} %bitcast.347, bf16[4,256,512]{2,1,0:T(8,128)(2,1)S(1)} %bitcast.315), kind=kOutput, calls=%fused_computation.3 | convolution fusion | flops 1101004800 | bytes 36700160 | tf_op jit(solution)/shard_map/ynq,nqd->ynd/dot_general | solution.py:40
  178.9 5.0 %fusion.120 = f32[4,1024,256]{1,2,0:T(8,128)S(1)} fusion(bf16[4,256,512]{2,1,0:T(8,128)(2,1)S(1)} %bitcast.314, bf16[1024,4,512]{0,2,1:T(8,128)(2,1)} %get-tuple-element.29), kind=kOutput, calls=%fused_computation.155 | convolution fusion | flops 1073741824 | bytes 9437184 | tf_op jit(solution)/shard_map/eaq,awq->eaw/dot_general | solution.py:52
  183.9 3.4 convolution_add_fusion
  187.3 5.4 %copy.158 = f32[1024,1024]{1,0:T(8,128)} copy(f32[1024,1024]{0,1:T(8,128)} %bitcast.323) | data formatting | bytes 8388608 | tf_op jit(solution)/shard_map/add | solution.py:214
  192.7 3.6 fusion.26
  197.3 4.5 %fusion.25 = (bf16[1024,1024]{1,0:T(8,128)(2,1)S(1)}, bf16[1024,1024]{1,0:T(8,128)(2,1)}) fusion(bf16[1024,1024]{1,0:T(8,128)(2,1)S(1)} %copy-done.3, f32[1024,1024]{1,0:T(8,128)S(1)} %copy-done.10, bf16[1,1024,1024]{2,1,0:T(8,128)(2,1)} %param.16, f32[1024]{0:T(1024)S(1)} %broadcast_multiply_fusion, f32[1024]{0:T(1024)S(1)} %get-tuple-element.37, ...), kind=kLoop, calls=%fused_computation.44 | loop fusion | flops 13631488 | bytes 14700544 | tf_op jit(solution)/shard_map/convert_element_type | solution.py:23
  208.9 4.2 %copy.161 = bf16[8,128,1024]{2,0,1:T(8,128)(2,1)} copy(bf16[8,128,1024]{1,2,0:T(8,128)(2,1)} %convert_bitcast_fusion.1) | data formatting | bytes 4194304 | tf_op jit(solution)/shard_map/convert_element_type | solution.py:226
  213.2 4.4 %all-to-all-start.4 = ((bf16[8,128,1024]{2,0,1:T(8,128)(2,1)}), bf16[8,128,1024]{2,0,1:T(8,128)(2,1)}, u32[]{:S(2)}, u32[]{:S(2)}) async-start(bf16[8,128,1024]{2,0,1:T(8,128)(2,1)} %copy.161), calls=%async_computation.4 | async-start | bytes 4194304 | tf_op jit(solution)/shard_map/all_to_all | solution.py:227
  217.6 7.6 %fusion.42 = bf16[1024,4,4,128]{0,3,1,2:T(8,128)(2,1)S(1)} fusion(f32[1024,4,4,128]{0,3,2,1:T(8,128)} %bitcast.344, f32[1024,4,4,128]{0,3,2,1:T(8,128)} %bitcast.320), kind=kLoop, calls=%fused_computation.73 | loop fusion | flops 12582912 | bytes 20971520 | tf_op jit(solution)/shard_map/transpose | solution.py:76
  226.8 2.3 multiply_convert_fusion.9
  229.1 6.3 %fusion.56 = f32[4,1024,512]{1,2,0:T(8,128)} fusion(bf16[4,256,512]{2,1,0:T(8,128)(2,1)S(1)} %bitcast.313, bf16[128,4,8,256]{3,2,1,0:T(8,128)(2,1)} %bitcast.324), kind=kOutput, calls=%fused_computation.87 | convolution fusion | flops 1073741824 | bytes 11534336 | tf_op jit(solution)/shard_map/ynq,nqd->ynd/dot_general | solution.py:40
  235.5 4.6 %fusion.58 = f32[4,1024,512]{1,2,0:T(8,128)} fusion(bf16[4,256,512]{2,1,0:T(8,128)(2,1)S(1)} %bitcast.337, bf16[128,4,8,256]{3,2,1,0:T(8,128)(2,1)S(1)} %bitcast.325), kind=kOutput, calls=%fused_computation.89 | convolution fusion | flops 1073741824 | bytes 11534336 | tf_op jit(solution)/shard_map/ynq,nqd->ynd/dot_general | solution.py:40
  240.0 5.6 %all-to-all-done.4 = bf16[8,128,1024]{2,0,1:T(8,128)(2,1)} async-done(((bf16[8,128,1024]{2,0,1:T(8,128)(2,1)}), bf16[8,128,1024]{2,0,1:T(8,128)(2,1)}, u32[]{:S(2)}, u32[]{:S(2)}) %all-to-all-start.4) | async-done | bytes 2097184 | tf_op jit(solution)/shard_map/all_to_all | solution.py:227
  245.6 2.5 fusion.60
  248.1 2.9 convert_bitcast_fusion
  251.0 2.5 copy.166
  253.5 4.4 %all-to-all-start.5 = ((bf16[64,16,1024]{2,1,0:T(8,128)(2,1)}), bf16[64,16,1024]{2,1,0:T(8,128)(2,1)}, u32[]{:S(2)}, u32[]{:S(2)}) async-start(bf16[64,16,1024]{2,1,0:T(8,128)(2,1)} %copy.166), calls=%async_computation.5 | async-start | bytes 4194304 | tf_op jit(solution)/shard_map/all_to_all | solution.py:234
  258.0 9.6 %fusion.41 = bf16[1024,4,4,128]{0,3,1,2:T(8,128)(2,1)} fusion(f32[1024,4,4,128]{0,3,2,1:T(8,128)} %bitcast.321, f32[1024,4,4,128]{0,3,2,1:T(8,128)} %bitcast.322), kind=kLoop, calls=%fused_computation.72 | loop fusion | flops 12582912 | bytes 20971520 | tf_op jit(solution)/shard_map/transpose | solution.py:76
  268.3 3.3 copy.208
  271.6 5.4 %copy.204 = f32[8,128,1024]{2,1,0:T(8,128)} copy(f32[8,128,1024]{1,0,2:T(8,128)} %bitcast.334) | data formatting | bytes 8388608 | tf_op jit(solution)/shard_map/reshape | solution.py:58
  277.0 5.4 %copy.170 = f32[1024,1024]{1,0:T(8,128)} copy(f32[1024,1024]{0,1:T(8,128)} %bitcast.319) | data formatting | bytes 8388608 | tf_op jit(solution)/shard_map/reshape | solution.py:58
  282.4 7.5 %copy.137 = bf16[1024,4,4,128]{3,2,0,1:T(4,128)(2,1)} copy(bf16[1024,4,4,128]{0,3,1,2:T(8,128)(2,1)} %fusion.41) | data formatting | bytes 8388608 | tf_op jit(solution)/shard_map/transpose | solution.py:76
  289.9 7.2 %reshape_reshape.6 = bf16[1024,4,512]{2,0,1:T(8,128)(2,1)} reshape(bf16[1024,4,4,128]{3,2,0,1:T(4,128)(2,1)} %copy.137) | data formatting | bytes 8388608 | tf_op jit(solution)/shard_map/reshape;reshape | solution.py:42
  297.1 5.8 %fusion.118 = f32[4,1024,256]{1,2,0:T(8,128)} fusion(bf16[1024,4,512]{2,0,1:T(8,128)(2,1)} %reshape_reshape.6, bf16[4,512,256]{2,1,0:T(8,128)(2,1)} %bitcast.354), kind=kOutput, calls=%fused_computation.153 | convolution fusion | flops 1073741824 | bytes 9437184 | tf_op jit(solution)/shard_map/ynq,nqd->ynd/dot_general | solution.py:40
  302.9 5.3 %copy.139 = f32[1024,1024]{1,0:T(8,128)} copy(f32[1024,1024]{0,1:T(8,128)} %bitcast.333) | data formatting | bytes 8388608 | tf_op jit(solution)/shard_map/reshape | solution.py:46
  308.2 5.1 %fusion.51 = bf16[1,1024,1024]{2,1,0:T(8,128)(2,1)} fusion(f32[1024,1024]{1,0:T(8,128)} %copy.139, bf16[1024,1024]{1,0:T(8,128)(2,1)} %copy-done.16), kind=kLoop, calls=%fused_computation.82 | loop fusion | flops 3145728 | bytes 8388608 | tf_op jit(solution)/shard_map/broadcast_in_dim | solution.py:193
  313.4 5.5 %collective-permute-start = (bf16[1,1024,1024]{2,1,0:T(8,128)(2,1)}, bf16[1,1024,1024]{2,1,0:T(8,128)(2,1)}, u32[]{:S(2)}, u32[]{:S(2)}) collective-permute-start(bf16[1,1024,1024]{2,1,0:T(8,128)(2,1)} %fusion.51), channel_id=1, source_target_pairs={{0,8},{8,16},{16,24},{1,9},{9,17},{17,25},{2,10},{10,18},{18,26},{... | collective-permute-start | bytes 6291464 | tf_op jit(solution)/shard_map/ppermute | solution.py:19
  324.0 3.6 fusion.36
  328.3 3.0 fusion.15
  332.9 2.3 multiply_convert_fusion.11
  335.2 4.2 %fusion.46 = bf16[1,64,16,1024]{3,1,2,0:T(8,128)(2,1)S(1)} fusion(f32[16,1024,64]{1,2,0:T(8,128)} %copy-done.11, f32[16,1024,64]{1,2,0:T(8,128)} %copy-done.12), kind=kLoop, calls=%fused_computation.79 | loop fusion | flops 2097152 | bytes 10485760 | tf_op jit(solution)/shard_map/broadcast_in_dim | solution.py:265
  339.4 2.5 copy.179
  341.9 21.3 %collective-permute-done = bf16[1,1024,1024]{2,1,0:T(8,128)(2,1)} collective-permute-done((bf16[1,1024,1024]{2,1,0:T(8,128)(2,1)}, bf16[1,1024,1024]{2,1,0:T(8,128)(2,1)}, u32[]{:S(2)}, u32[]{:S(2)}) %collective-permute-start) | collective-permute-done | bytes 2097184 | tf_op jit(solution)/shard_map/ppermute | solution.py:19
  363.1 17.9 %collective-permute-done.1 = bf16[1,1024,1024]{2,1,0:T(8,128)(2,1)} collective-permute-done((bf16[1,1024,1024]{2,1,0:T(8,128)(2,1)}, bf16[1,1024,1024]{2,1,0:T(8,128)(2,1)}, u32[]{:S(2)}, u32[]{:S(2)}) %collective-permute-start.1) | collective-permute-done | bytes 2097184 | tf_op jit(solution)/shard_map/ppermute | solution.py:19
  381.0 15.7 %reduce-scatter.7.cloned.1.call-done = bf16[128,512]{1,0:T(8,128)(2,1)} async-done(((bf16[1024,512]{1,0:T(8,128)(2,1)}), bf16[128,512]{1,0:T(8,128)(2,1)}) %reduce-scatter.7.cloned.1.call-update) | async-done | bytes 131088 | tf_op jit(solution)/shard_map/reduce_scatter | solution.py:252
  396.7 3.1 copy.261
  399.8 3.1 copy.262
  (135 shorter events, 43.8 us)
Async XLA Ops:
  7.2 158.3 %copy-start = (bf16[1,1024,512]{2,1,0:T(8,128)(2,1)S(1)}, bf16[1,1024,512]{2,1,0:T(8,128)(2,1)}, u32[]{:S(2)}) copy-start(bf16[1,1024,512]{2,1,0:T(8,128)(2,1)} %param.25) | copy-start | bytes 3145732
  7.2 4.3 %copy-start.36 = (bf16[1,8,128,128]{3,2,1,0:T(8,128)(2,1)S(1)}, bf16[1,8,128,128]{3,2,1,0:T(8,128)(2,1)}, u32[]{:S(2)}) copy-start(bf16[1,8,128,128]{3,2,1,0:T(8,128)(2,1)} %param.19) | copy-start | bytes 786436
  7.2 4.3 %copy-start.43 = (f32[1,1024]{1,0:T(1,128)S(1)}, f32[1,1024]{1,0:T(1,128)}, u32[]{:S(2)}) copy-start(f32[1,1024]{1,0:T(1,128)} %param.17) | copy-start | bytes 12292
  13.9 9.5 %copy-start.1 = (bf16[1,1024,1024]{2,1,0:T(8,128)(2,1)S(1)}, bf16[1,1024,1024]{2,1,0:T(8,128)(2,1)}, u32[]{:S(2)}) copy-start(bf16[1,1024,1024]{2,1,0:T(8,128)(2,1)} %param.15) | copy-start | bytes 6291460
  18.2 31.9 %all-to-all-start = ((bf16[8,128,1024]{2,0,1:T(8,128)(2,1)}), bf16[8,128,1024]{2,0,1:T(8,128)(2,1)}, u32[]{:S(2)}, u32[]{:S(2)}) async-start(bf16[8,128,1024]{2,0,1:T(8,128)(2,1)} %copy.122), calls=%async_computation | async-start | bytes 4194304 | tf_op jit(solution)/shard_map/all_to_all | solution.py:172
  23.8 2.1 copy-start.4
  32.4 26.4 %copy-start.39 = (bf16[1,16,64,64]{3,2,1,0:T(8,128)(2,1)S(1)}, bf16[1,16,64,64]{3,2,1,0:T(8,128)(2,1)}, u32[]{:S(2)}) copy-start(bf16[1,16,64,64]{3,2,1,0:T(8,128)(2,1)} %param.22) | copy-start | bytes 393220
  50.1 31.2 %all-to-all-start.2 = ((bf16[8,128,1024]{2,0,1:T(8,128)(2,1)}), bf16[8,128,1024]{2,0,1:T(8,128)(2,1)}, u32[]{:S(2)}, u32[]{:S(2)}) async-start(bf16[8,128,1024]{2,0,1:T(8,128)(2,1)} %copy.141), calls=%async_computation.2 | async-start | bytes 4194304 | tf_op jit(solution)/shard_map/all_to_all | solution.py:173
  81.3 31.3 %all-to-all-start.1 = ((bf16[64,16,1024]{2,1,0:T(8,128)(2,1)}), bf16[64,16,1024]{2,1,0:T(8,128)(2,1)}, u32[]{:S(2)}, u32[]{:S(2)}) async-start(bf16[64,16,1024]{2,1,0:T(8,128)(2,1)} %copy.127), calls=%async_computation.1 | async-start | bytes 4194304 | tf_op jit(solution)/shard_map/all_to_all | solution.py:178
  98.8 5.3 %copy-start.41 = (bf16[1,16,64,64]{3,2,1,0:T(8,128)(2,1)S(1)}, bf16[1,16,64,64]{3,2,1,0:T(8,128)(2,1)}, u32[]{:S(2)}) copy-start(bf16[1,16,64,64]{3,2,1,0:T(8,128)(2,1)} %param.20) | copy-start | bytes 393220
  104.2 2.4 copy-start.20
  106.6 2.8 copy-start.11
  112.6 36.3 %all-to-all-start.3 = ((bf16[64,16,1024]{2,1,0:T(8,128)(2,1)}), bf16[64,16,1024]{2,1,0:T(8,128)(2,1)}, u32[]{:S(2)}, u32[]{:S(2)}) async-start(bf16[64,16,1024]{2,1,0:T(8,128)(2,1)} %copy.144), calls=%async_computation.3 | async-start | bytes 4194304 | tf_op jit(solution)/shard_map/all_to_all | solution.py:179
  117.0 264.0 %reduce-scatter.5.cloned.1.call-start = ((), (), s32[]{:S(2)}) async-start(), calls=%async_computation.10 | async-start | bytes 589824 | tf_op jit(solution)/shard_map/reduce_scatter | solution.py:249
  141.1 2.0 copy-start.38
  143.0 1.6 copy-start.14
  143.0 2.8 copy-start.23
  147.1 1.4 copy-start.16
  150.8 2.2 copy-start.6
  152.9 2.2 copy-start.8
  152.9 3.5 copy-start.44
  155.2 1.3 copy-start.2
  165.5 13.4 %copy-start.15 = (f32[4,1024,512]{1,2,0:T(8,128)}, f32[4,1024,512]{1,2,0:T(8,128)S(1)}, u32[]{:S(2)}) copy-start(f32[4,1024,512]{1,2,0:T(8,128)S(1)} %fusion.119) | copy-start | bytes 25165828
  178.9 5.0 %copy-start.27 = (bf16[1024,4,512]{0,2,1:T(8,128)(2,1)}, bf16[1024,4,512]{0,2,1:T(8,128)(2,1)S(1)}, u32[]{:S(2)}) copy-start(bf16[1024,4,512]{0,2,1:T(8,128)(2,1)S(1)} %get-tuple-element.28) | copy-start | bytes 12582916
  178.9 5.0 %copy-start.25 = (bf16[1,1024,512]{2,1,0:T(8,128)(2,1)S(1)}, bf16[1,1024,512]{2,1,0:T(8,128)(2,1)}, u32[]{:S(2)}) copy-start(bf16[1,1024,512]{2,1,0:T(8,128)(2,1)} %param.26) | copy-start | bytes 3145732
  192.7 3.6 copy-start.3
  192.7 4.7 %copy-start.10 = (f32[1024,1024]{1,0:T(8,128)S(1)}, f32[1024,1024]{1,0:T(8,128)}, u32[]{:S(2)}) copy-start(f32[1024,1024]{1,0:T(8,128)} %copy.158) | copy-start | bytes 12582916
  197.3 4.5 %copy-start.7 = (f32[1024,1024]{1,0:T(8,128)S(1)}, f32[1024,1024]{1,0:T(8,128)}, u32[]{:S(2)}) copy-start(f32[1024,1024]{1,0:T(8,128)} %copy.149) | copy-start | bytes 12582916
  197.3 5.5 %copy-start.9 = (f32[8,1024,128]{1,2,0:T(8,128)S(1)}, f32[8,1024,128]{1,2,0:T(8,128)}, u32[]{:S(2)}) copy-start(f32[8,1024,128]{1,2,0:T(8,128)} %copy-done.8) | copy-start | bytes 12582916
  201.9 2.5 copy-start.17
  202.8 2.2 copy-start.22
  204.3 2.4 copy-start.30
  213.2 32.4 %all-to-all-start.4 = ((bf16[8,128,1024]{2,0,1:T(8,128)(2,1)}), bf16[8,128,1024]{2,0,1:T(8,128)(2,1)}, u32[]{:S(2)}, u32[]{:S(2)}) async-start(bf16[8,128,1024]{2,0,1:T(8,128)(2,1)} %copy.161), calls=%async_computation.4 | async-start | bytes 4194304 | tf_op jit(solution)/shard_map/all_to_all | solution.py:227
  217.5 163.5 %reduce-scatter.11.cloned.1.call-start = ((), (), s32[]{:S(2)}) async-start(), calls=%async_computation.13 | async-start | bytes 1179648 | tf_op jit(solution)/shard_map/reduce_scatter | solution.py:258
  225.2 1.6 copy-start.29
  229.1 6.3 %copy-start.19 = (bf16[1024,1024]{1,0:T(8,128)(2,1)S(1)}, bf16[1024,1024]{1,0:T(8,128)(2,1)}, u32[]{:S(2)}) copy-start(bf16[1024,1024]{1,0:T(8,128)(2,1)} %get-tuple-element.36) | copy-start | bytes 6291460
  229.1 6.3 %copy-start.26 = (bf16[1,1024,512]{2,1,0:T(8,128)(2,1)S(1)}, bf16[1,1024,512]{2,1,0:T(8,128)(2,1)}, u32[]{:S(2)}) copy-start(bf16[1,1024,512]{2,1,0:T(8,128)(2,1)} %param.26) | copy-start | bytes 3145732
  235.5 10.1 %copy-start.40 = (bf16[1,16,64,64]{3,2,1,0:T(8,128)(2,1)S(1)}, bf16[1,16,64,64]{3,2,1,0:T(8,128)(2,1)}, u32[]{:S(2)}) copy-start(bf16[1,16,64,64]{3,2,1,0:T(8,128)(2,1)} %param.22) | copy-start | bytes 393220
  245.6 2.5 copy-start.21
  245.6 2.5 copy-start.42
  248.1 2.9 copy-start.12
  253.5 67.7 %all-to-all-start.5 = ((bf16[64,16,1024]{2,1,0:T(8,128)(2,1)}), bf16[64,16,1024]{2,1,0:T(8,128)(2,1)}, u32[]{:S(2)}, u32[]{:S(2)}) async-start(bf16[64,16,1024]{2,1,0:T(8,128)(2,1)} %copy.166), calls=%async_computation.5 | async-start | bytes 4194304 | tf_op jit(solution)/shard_map/all_to_all | solution.py:234
  257.9 123.1 %reduce-scatter.9.cloned.1.call-start = ((), (), s32[]{:S(2)}) async-start(), calls=%async_computation.12 | async-start | bytes 1179648 | tf_op jit(solution)/shard_map/reduce_scatter | solution.py:255
  257.9 9.6 %copy-start.31 = (bf16[1024,1024]{1,0:T(8,128)(2,1)S(1)}, bf16[1024,1024]{1,0:T(8,128)(2,1)}, u32[]{:S(2)}) copy-start(bf16[1024,1024]{1,0:T(8,128)(2,1)} %copy-done.30) | copy-start | bytes 6291460
  257.9 9.6 %copy-start.34 = (bf16[1,1024,256]{2,1,0:T(8,128)(2,1)S(1)}, bf16[1,1024,256]{2,1,0:T(8,128)(2,1)}, u32[]{:S(2)}) copy-start(bf16[1,1024,256]{2,1,0:T(8,128)(2,1)} %param.24) | copy-start | bytes 1572868
  268.3 3.3 copy-start.13
  308.2 10.6 %copy-start.28 = (bf16[1024,4,512]{0,2,1:T(8,128)(2,1)S(1)}, bf16[1024,4,512]{0,2,1:T(8,128)(2,1)}, u32[]{:S(2)}) copy-start(bf16[1024,4,512]{0,2,1:T(8,128)(2,1)} %copy-done.27) | copy-start | bytes 12582916
  308.2 10.6 %copy-start.32 = (bf16[1024,1024]{0,1:T(8,128)(2,1)S(1)}, bf16[1024,1024]{0,1:T(8,128)(2,1)}, u32[]{:S(2)}) copy-start(bf16[1024,1024]{0,1:T(8,128)(2,1)} %copy.205) | copy-start | bytes 6291460
  313.4 49.8 %collective-permute-start = (bf16[1,1024,1024]{2,1,0:T(8,128)(2,1)}, bf16[1,1024,1024]{2,1,0:T(8,128)(2,1)}, u32[]{:S(2)}, u32[]{:S(2)}) collective-permute-start(bf16[1,1024,1024]{2,1,0:T(8,128)(2,1)} %fusion.51), channel_id=1, source_target_pairs={{0,8},{8,16},{16,24},{1,9},{9,17},{17,25},{2,10},{10,18},{18,26},{... | collective-permute-start | bytes 6291464 | tf_op jit(solution)/shard_map/ppermute | solution.py:19
  321.1 2.0 copy-start.37
  321.1 75.6 %reduce-scatter.7.cloned.1.call-start = ((), (), s32[]{:S(2)}) async-start(), calls=%async_computation.11 | async-start | bytes 1179648 | tf_op jit(solution)/shard_map/reduce_scatter | solution.py:252
  321.2 2.8 copy-start.5
  324.0 3.7 copy-start.18
  324.0 4.3 %copy-start.24 = (f32[1024,1024]{1,0:T(8,128)S(1)}, f32[1024,1024]{1,0:T(8,128)}, u32[]{:S(2)}) copy-start(f32[1024,1024]{1,0:T(8,128)} %copy.170) | copy-start | bytes 12582916
  324.0 4.3 %copy-start.45 = (f32[1024]{0:T(1024)S(1)}, f32[1024]{0:T(1024)}, u32[]{:S(2)}) copy-start(f32[1024]{0:T(1024)} %get-tuple-element.32) | copy-start | bytes 12292
  328.3 4.6 %copy-start.33 = (bf16[1024,1024]{0,1:T(8,128)(2,1)S(1)}, bf16[1024,1024]{0,1:T(8,128)(2,1)}, u32[]{:S(2)}) copy-start(bf16[1024,1024]{0,1:T(8,128)(2,1)} %copy.205) | copy-start | bytes 6291460
  328.3 4.6 %copy-start.35 = (bf16[1024,4,512]{0,2,1:T(8,128)(2,1)S(1)}, bf16[1024,4,512]{0,2,1:T(8,128)(2,1)}, u32[]{:S(2)}) copy-start(bf16[1024,4,512]{0,2,1:T(8,128)(2,1)} %get-tuple-element.29) | copy-start | bytes 12582916
  331.3 49.7 %collective-permute-start.1 = (bf16[1,1024,1024]{2,1,0:T(8,128)(2,1)}, bf16[1,1024,1024]{2,1,0:T(8,128)(2,1)}, u32[]{:S(2)}, u32[]{:S(2)}) collective-permute-start(bf16[1,1024,1024]{2,1,0:T(8,128)(2,1)} %bitcast.86), channel_id=1, source_target_pairs={{8,0},{16,8},{24,16},{9,1},{17,9},{25,17},{10,2},{18,10},{26,18},{... | collective-permute-start | bytes 6291464 | tf_op jit(solution)/shard_map/ppermute | solution.py:19
Sparse Core Ops, SparseCore 0:
  213.3 38.6 reduce-scatter.4
  256.0 39.4 reduce-scatter.10
  321.2 35.4 reduce-scatter.8
  360.6 36.0 reduce-scatter.6
where the time goes:
time: 416 us; the launch traced here: 410 us
  local copies, waits for them, and re-layouts  124 us (30%)
  matrix products  96.6 us (23%)
  waiting for transfers between devices  88 us (21%)
  other arithmetic  51.3 us (12%)
  starting transfers between devices  34.7 us (8%)
  between operations  14.9 us (4%)
    dot_general x7, matrix products, block_apply(): jnp.einsum('ynq,nqd->ynd', value_array.reshape(item_count, block_list, -1...  43.8 us
    ppermute x2, waiting for transfers between devices, from_behind(): return lax.ppermute(array, axis, pairs)  39.2 us
    unnamed x97, local copies, waits for them, and re-layouts  25 us
    all_to_all x1, waiting for transfers between devices, shards(): lax.all_to_all(folded_fwd, 'seq', split_axis=1, concat_axis=0, tiled=True)  17.7 us
    transpose x2, other arithmetic, shuffle(): return value_array.reshape(item_count, block_list, block_list, -1).transp...  17.2 us
    reshape x3, local copies, waits for them, and re-layouts, block_apply(): return final_output.reshape(item_count, -1)  16.5 us
    reduce_scatter x1, waiting for transfers between devices, shards(): lax.psum_scatter(term_up.astype(jnp.bfloat16), 'seq', scatter_dimension=0...  15.7 us
    dot_general x4, matrix products, block_back(): jnp.einsum('eaq,awq->eaw', incoming_gradient.reshape(item_count, block_li...  12.4 us
  transfers between devices with their start and end apart: 12, of which 7 were waited for; matrix products, arithmetic and copies ran while one was open for 45% of the time, Pallas kernels for 0%

commit v1 on v0

v1 whole, which is shorter than its diff:
```python
import functools
import math

import jax
import jax.numpy as jnp
from jax import lax
from jax.experimental import pallas as pl
from jax.experimental.pallas import tpu as pltpu
from jax.sharding import PartitionSpec as P

NB = 4
EPS = 1e-06
F32 = jnp.float32
BF16 = jnp.bfloat16
MIB = 1024 * 1024


def dot(a, b):
    return jnp.dot(a, b, preferred_element_type=F32)


def dot_t(a, b):
    return lax.dot_general(a, b, (((1,), (1,)), ((), ())), preferred_element_type=F32)


def t_dot(a, b):
    return lax.dot_general(a, b, (((0,), (0,)), ((), ())), preferred_element_type=F32)


def rms_scale(v):
    return lax.rsqrt(jnp.mean(v * v, axis=-1, keepdims=True) + EPS)


def norm_back(v, scale, gain, grad):
    scaled = gain * grad
    return scale * scaled - v * (scale * scale * scale) * jnp.mean(
        scaled * v, axis=-1, keepdims=True
    )


def cols_of(array, b, width):
    return array[:, b * width : (b + 1) * width]


def params(mib, steps=1):
    return pltpu.CompilerParams(
        dimension_semantics=("arbitrary",) * steps, vmem_limit_bytes=mib * MIB
    )


def cost(flops, nbytes):
    return pl.CostEstimate(flops=int(flops), bytes_accessed=int(nbytes), transcendentals=0)


class Sizes:
    def __init__(self, n, rows, cols, width):
        self.n = n
        self.rows = rows
        self.cols = cols
        self.width = width
        self.line = n * cols
        self.tall = n * rows
        self.tokens = rows * self.line
        self.per = 2 if rows % 2 == 0 else 1
        self.aligned = cols % 16 == 0

    def sent_shape(self):
        if self.aligned:
            return (self.n, self.rows, self.cols, self.width)
        return (self.rows, self.line, self.width)

    def sent_spec(self):
        if self.aligned:
            return pl.BlockSpec(
                (self.n, self.per, self.cols, self.width), lambda i: (0, i, 0, 0)
            )
        return pl.BlockSpec((self.per, self.line, self.width), lambda i: (i, 0, 0))

    def put(self, ref, r, value):
        if self.aligned:
            ref[:, r] = value.reshape(self.n, self.cols, self.width)
        else:
            ref[r] = value

    def get(self, ref, r):
        if self.aligned:
            return ref[:, r].reshape(self.line, self.width)
        return ref[r]

    def to_columns(self, array):
        if not self.aligned:
            array = array.reshape(self.rows, self.n, self.cols, self.width).transpose(1, 0, 2, 3)
        array = lax.all_to_all(array, "seq", split_axis=0, concat_axis=0, tiled=True)
        return array.reshape(self.tall * self.cols, self.width)

    def to_rows(self, array):
        array = array.reshape(self.n, self.rows, self.cols, self.width)
        array = lax.all_to_all(array, "seq", split_axis=0, concat_axis=0, tiled=True)
        if not self.aligned:
            array = array.transpose(1, 0, 2, 3).reshape(self.rows, self.line, self.width)
        return array

    def token_spec(self, width):
        return pl.BlockSpec((self.per * self.line, width), lambda i: (i, 0))

    def factor_spec(self):
        return pl.BlockSpec((self.per, self.line, self.line), lambda i: (i, 0, 0))


def whole(shape):
    return pl.BlockSpec(shape, lambda i: (0,) * len(shape))


def front_kernel(sz, x_ref, gain_ref, first_ref, sent_ref):
    for r in range(sz.per):
        x = x_ref[pl.ds(r * sz.line, sz.line), :].astype(F32)
        normed = (x * rms_scale(x) * gain_ref[...]).astype(BF16)
        sz.put(sent_ref, r, dot(first_ref[r], normed).astype(BF16))


def front(sz, x, gain, first):
    return pl.pallas_call(
        functools.partial(front_kernel, sz),
        grid=(sz.rows // sz.per,),
        in_specs=[sz.token_spec(sz.width), whole((1, sz.width)), sz.factor_spec()],
        out_specs=sz.sent_spec(),
        out_shape=jax.ShapeDtypeStruct(sz.sent_shape(), BF16),
        compiler_params=params(16),
        cost_estimate=cost(2 * sz.tokens * sz.line * sz.width, 4 * sz.tokens * sz.width),
        name="front",
    )(x, gain, first)


def expand_kernel(cols, tall, thin_ref, wide_ref):
    size = tall * cols
    pick = lax.broadcasted_iota(jnp.int32, (tall, size), 1) // cols
    pick = (pick == lax.broadcasted_iota(jnp.int32, (tall, size), 0)).astype(F32).astype(BF16)
    spread = dot(thin_ref[0], pick)
    left = lax.broadcasted_iota(jnp.int32, (size, size), 0) % cols
    right = lax.broadcasted_iota(jnp.int32, (size, size), 1) % cols
    wide_ref[0] = jnp.where(left == right, spread, 0.0).astype(BF16)


def expand(sz, second, third):
    size = sz.tall * sz.cols
    thin = jnp.stack(
        [
            second.transpose(1, 0, 2).reshape(size, sz.tall),
            third.transpose(1, 0, 2).reshape(size, sz.tall),
            third.transpose(2, 0, 1).reshape(size, sz.tall),
            second.transpose(2, 0, 1).reshape(size, sz.tall),
        ]
    )
    return pl.pallas_call(
        functools.partial(expand_kernel, sz.cols, sz.tall),
        grid=(4,),
        in_specs=[pl.BlockSpec((1, size, sz.tall), lambda i: (i, 0, 0))],
        out_specs=pl.BlockSpec((1, size, size), lambda i: (i, 0, 0)),
        out_shape=jax.ShapeDtypeStruct((4, size, size), BF16),
        compiler_params=params(32),
        cost_estimate=cost(8 * size * size * sz.tall, 8 * size * size),
        name="expand",
    )(thin)


def middle_kernel(x_ref, second_ref, third_ref, spectrum_ref, out_ref, *mixed_ref):
    mixed = dot(second_ref[0], x_ref[...])
    if mixed_ref:
        mixed_ref[0][...] = mixed
    filtered = (mixed * spectrum_ref[...].astype(F32)).astype(BF16)
    out_ref[...] = dot(third_ref[0], filtered).astype(BF16)


def middle(sz, x, wide, spectrum, keep):
    size = sz.tall * sz.cols
    part = 256
    strip = pl.BlockSpec((size, part), lambda i: (0, i))
    shapes = [jax.ShapeDtypeStruct((size, sz.width), BF16)]
    if keep:
        shapes.append(jax.ShapeDtypeStruct((size, sz.width), F32))
    return pl.pallas_call(
        middle_kernel,
        grid=(sz.width // part,),
        in_specs=[
            strip,
            pl.BlockSpec((1, size, size), lambda i: (0, 0, 0)),
            pl.BlockSpec((1, size, size), lambda i: (1, 0, 0)),
            strip,
        ],
        out_specs=[strip] * len(shapes),
        out_shape=shapes,
        compiler_params=params(28),
        cost_estimate=cost(4 * size * size * sz.width, 10 * size * sz.width),
        name="middle",
    )(x, wide, wide, spectrum)


def middle_back_kernel(
    d_ref, third_ref, second_ref, spectrum_ref, mixed_ref, out_ref, grad_ref
):
    d_filtered = dot(third_ref[0], d_ref[...])
    grad_ref[...] = (d_filtered * mixed_ref[...]).astype(BF16)
    d_mixed = (d_filtered * spectrum_ref[...].astype(F32)).astype(BF16)
    out_ref[...] = dot(second_ref[0], d_mixed).astype(BF16)


def middle_back(sz, d, wide, spectrum, mixed):
    size = sz.tall * sz.cols
    part = 256
    strip = pl.BlockSpec((size, part), lambda i: (0, i))
    return pl.pallas_call(
        middle_back_kernel,
        grid=(sz.width // part,),
        in_specs=[
            strip,
            pl.BlockSpec((1, size, size), lambda i: (2, 0, 0)),
            pl.BlockSpec((1, size, size), lambda i: (3, 0, 0)),
            strip,
            strip,
        ],
        out_specs=[strip, strip],
        out_shape=[jax.ShapeDtypeStruct((size, sz.width), BF16)] * 2,
        compiler_params=params(28),
        cost_estimate=cost(4 * size * size * sz.width, 12 * size * sz.width),
        name="middle_back",
    )(d, wide, wide, spectrum, mixed)


def tail_front(sz, x_ref, b1_ref, fourth_ref, gain_one, mix_ref):
    x = x_ref[...].astype(F32)
    normed = (x * rms_scale(x) * gain_one).astype(BF16)
    collected = [dot(fourth_ref[r], sz.get(b1_ref, r)) for r in range(sz.per)]
    back = collected[0] if sz.per == 1 else jnp.concatenate(collected, axis=0)
    wide = sz.width // NB
    gate = jnp.concatenate(
        [
            dot(cols_of(normed, b, wide), mix_ref[b * wide : (b + 1) * wide, :])
            for b in range(NB)
        ],
        axis=1,
    )
    y1 = (x + back * gate).astype(BF16)
    return normed, back, gate, y1


def tail_kernel(
    sz,
    x_ref,
    b1_ref,
    fourth_ref,
    gain_one_ref,
    gain_two_ref,
    mix_ref,
    up_ref,
    act_ref,
    down_ref,
    out_ref,
):
    _, _, _, y1 = tail_front(sz, x_ref, b1_ref, fourth_ref, gain_one_ref[...], mix_ref)
    y = y1.astype(F32)
    n2 = (y * rms_scale(y) * gain_two_ref[...]).astype(BF16)
    wide = sz.width // NB
    hidden = []
    for b in range(NB):
        rows = slice(b * wide, (b + 1) * wide)
        lifted = dot(n2[:, rows], up_ref[rows, :])
        gated = dot(n2[:, rows], act_ref[rows, :])
        hidden.append((gated * jax.nn.sigmoid(gated) * lifted).astype(BF16))
    units = hidden[0].shape[1]
    piece = units // NB
    for b in range(NB):
        mixed = jnp.concatenate([cols_of(h, b, piece) for h in hidden], axis=1)
        out_ref[:, b * wide : (b + 1) * wide] = (
            cols_of(y, b, wide) + dot(mixed, down_ref[b * units : (b + 1) * units, :])
        ).astype(BF16)


def tail_specs(sz, weights):
    return [
        sz.token_spec(sz.width),
        sz.sent_spec(),
        sz.factor_spec(),
        whole((1, sz.width)),
        whole((1, sz.width)),
    ] + [whole(w.shape) for w in weights]


def tail(sz, x, b1, fourth, gain_one, gain_two, *weights):
    return pl.pallas_call(
        functools.partial(tail_kernel, sz),
        grid=(sz.rows // sz.per,),
        in_specs=tail_specs(sz, weights),
        out_specs=sz.token_spec(sz.width),
        out_shape=jax.ShapeDtypeStruct((sz.tokens, sz.width), BF16),
        compiler_params=params(40),
        cost_estimate=cost(8 * sz.tokens * sz.width * sz.width // 2, 8 * sz.tokens * sz.width),
        name="tail",
    )(x, b1, fourth, gain_one, gain_two, *weights)


def turn_kernel(
    sz,
    x_ref,
    b1_ref,
    fourth_ref,
    gain_one_ref,
    gain_two_ref,
    mix_ref,
    up_ref,
    act_ref,
    down_ref,
    g_ref,
    sent_ref,
    dy_ref,
    dgate_ref,
    n1_ref,
    n2_ref,
    hs_ref,
    dup_ref,
    dact_ref,
):
    n1, back, gate, y1 = tail_front(sz, x_ref, b1_ref, fourth_ref, gain_one_ref[...], mix_ref)
    n1_ref[...] = n1
    y = y1.astype(F32)
    scale_two = rms_scale(y)
    n2 = (y * scale_two * gain_two_ref[...]).astype(BF16)
    n2_ref[...] = n2
    wide = sz.width // NB
    units = up_ref.shape[1]
    piece = units // NB
    d_shuffled = [
        dot_t(g_ref[:, b * wide : (b + 1) * wide], down_ref[b * units : (b + 1) * units, :]).astype(
            BF16
        )
        for b in range(NB)
    ]
    d_n2 = []
    for b in range(NB):
        rows = slice(b * wide, (b + 1) * wide)
        lifted = dot(n2[:, rows], up_ref[rows, :])
        gated = dot(n2[:, rows], act_ref[rows, :])
        sigma = jax.nn.sigmoid(gated)
        silu = gated * sigma
        hidden = (silu * lifted).astype(BF16)
        for k in range(NB):
            at = k * units + b * piece
            hs_ref[:, at : at + piece] = cols_of(hidden, k, piece)
        d_hidden = jnp.concatenate([cols_of(d, b, piece) for d in d_shuffled], axis=1).astype(F32)
        d_lift = (d_hidden * silu).astype(BF16)
        d_gated = (d_hidden * lifted * sigma * (1.0 + gated * (1.0 - sigma))).astype(BF16)
        dup_ref[:, b * units : (b + 1) * units] = d_lift
        dact_ref[:, b * units : (b + 1) * units] = d_gated
        d_n2.append(dot_t(d_lift, up_ref[rows, :]) + dot_t(d_gated, act_ref[rows, :]))
    d_n2 = jnp.concatenate(d_n2, axis=1)
    dy = (g_ref[...].astype(F32) + norm_back(y, scale_two, gain_two_ref[...], d_n2)).astype(BF16)
    dy_ref[...] = dy
    dyw = dy.astype(F32)
    dgate_ref[...] = (dyw * back).astype(BF16)
    d_back = (dyw * gate).astype(BF16)
    for r in range(sz.per):
        part = d_back[r * sz.line : (r + 1) * sz.line, :]
        sz.put(sent_ref, r, t_dot(fourth_ref[r], part).astype(BF16))


def turn(sz, x, b1, fourth, gain_one, gain_two, mix, up, act, down, g):
    weights = (mix, up, act, down)
    units = NB * up.shape[1]
    widths = [sz.width] * 4 + [units] * 3
    return pl.pallas_call(
        functools.partial(turn_kernel, sz),
        grid=(sz.rows // sz.per,),
        in_specs=tail_specs(sz, weights) + [sz.token_spec(sz.width)],
        out_specs=[sz.sent_spec()] + [sz.token_spec(w) for w in widths],
        out_shape=[jax.ShapeDtypeStruct(sz.sent_shape(), BF16)]
        + [jax.ShapeDtypeStruct((sz.tokens, w), BF16) for w in widths],
        compiler_params=params(48),
        cost_estimate=cost(8 * sz.tokens * sz.width * sz.width, 30 * sz.tokens * sz.width),
        name="turn",
    )(x, b1, fourth, gain_one, gain_two, *weights, g)


def weights_kernel(factor, share, n1, dgate, n2, dup, dact, hs, g, out_ref):
    wide = n1.shape[1]
    units = dup.shape[1]
    out_ref[:, :wide] = (t_dot(n1[...], dgate[...]) * factor).astype(BF16)
    out_ref[:, wide : wide + units] = (t_dot(n2[...], dup[...]) * factor).astype(BF16)
    out_ref[:, wide + units : wide + 2 * units] = (t_dot(n2[...], dact[...]) * factor).astype(BF16)
    down = (t_dot(hs[...], g[...]) * factor).astype(BF16)
    ratio = units // wide
    for k in range(units // share):
        at = wide + 2 * units + (k % ratio) * wide
        out_ref[(k // ratio) * share : (k // ratio + 1) * share, at : at + wide] = down[
            k * share : (k + 1) * share, :
        ]


def weight_grads(sz, factor, n1, dgate, n2, dup, dact, hs, g):
    wide = sz.width // NB
    units = dup.shape[1] // NB
    total = wide + 3 * units
    slim = pl.BlockSpec((sz.tokens, wide), lambda i: (0, i))
    broad = pl.BlockSpec((sz.tokens, units), lambda i: (0, i))
    return pl.pallas_call(
        functools.partial(weights_kernel, factor, sz.width // sz.n),
        grid=(NB,),
        in_specs=[slim, slim, slim, broad, broad, broad, slim],
        out_specs=pl.BlockSpec((wide, total), lambda i: (i, 0)),
        out_shape=jax.ShapeDtypeStruct((sz.width, total), BF16),
        compiler_params=params(32),
        cost_estimate=cost(2 * sz.tokens * sz.width * total, 24 * sz.tokens * sz.width),
        name="weight_grads",
    )(n1, dgate, n2, dup, dact, hs, g)


def last_kernel(sz, x_ref, d_ref, first_ref, gain_ref, mix_ref, dgate_ref, dy_ref, out_ref):
    wide = sz.width // NB
    gain = gain_ref[...]
    for r in range(sz.per):
        at = pl.ds(r * sz.line, sz.line)
        gated = jnp.concatenate(
            [
                dot_t(
                    dgate_ref[at, b * wide : (b + 1) * wide], mix_ref[b * wide : (b + 1) * wide, :]
                )
                for b in range(NB)
            ],
            axis=1,
        )
        d_normed = t_dot(first_ref[r], sz.get(d_ref, r)) + gated
        x = x_ref[at, :].astype(F32)
        out_ref[at, :] = (
            dy_ref[at, :].astype(F32) + norm_back(x, rms_scale(x), gain, d_normed)
        ).astype(BF16)


def last(sz, x, d, first, gain, mix, dgate, dy):
    tokens = sz.token_spec(sz.width)
    return pl.pallas_call(
        functools.partial(last_kernel, sz),
        grid=(sz.rows // sz.per,),
        in_specs=[
            tokens,
            sz.sent_spec(),
            sz.factor_spec(),
            whole((1, sz.width)),
            whole(mix.shape),
            tokens,
            tokens,
        ],
        out_specs=tokens,
        out_shape=jax.ShapeDtypeStruct((sz.tokens, sz.width), BF16),
        compiler_params=params(20),
        cost_estimate=cost(2 * sz.tokens * sz.width * 384, 10 * sz.tokens * sz.width),
        name="last",
    )(x, d, first, gain, mix, dgate, dy)


def shift(array, by):
    length = lax.axis_size("section")
    pairs = [(i, i + by) for i in range(length) if 0 <= i + by < length]
    return lax.ppermute(array, "section", pairs)


def shards(
    section_input,
    stashed_input,
    output_grad,
    gain_mixer,
    gain_channel,
    factor_first,
    factor_second,
    spectrum,
    factor_third,
    factor_fourth,
    mixer_gate,
    channel_up,
    channel_gate,
    channel_down,
):
    first = factor_first[0]
    fourth = factor_fourth[0]
    n = lax.axis_size("seq")
    rows = first.shape[0]
    cols = factor_second.shape[1]
    width = section_input.shape[2]
    sz = Sizes(n, rows, cols, width)
    size = sz.tall * cols
    kernel_here = spectrum[0].reshape(size, width)
    mix, up, act, down = mixer_gate[0], channel_up[0], channel_gate[0], channel_down[0]
    gain_one, gain_two = gain_mixer, gain_channel
    xa, xb, g = section_input[0], stashed_input[0], output_grad[0]
    factor = 1.0 / math.sqrt(sz.tall * sz.line)

    recv_b = sz.to_columns(front(sz, xb, gain_one, first))
    wide = expand(sz, factor_second[0], factor_third[0])
    sent_a = front(sz, xa, gain_one, first)
    sent_a, recv_b = lax.optimization_barrier((sent_a, recv_b))
    recv_a = sz.to_columns(sent_a)
    out_b, mixed_b = middle(sz, recv_b, wide, kernel_here, True)
    out_b, recv_a = lax.optimization_barrier((out_b, recv_a))
    rows_b = sz.to_rows(out_b)
    (out_a,) = middle(sz, recv_a, wide, kernel_here, False)
    out_a, rows_b = lax.optimization_barrier((out_a, rows_b))
    rows_a = sz.to_rows(out_a)

    sent, dy, dgate, n1, n2, hs, dup, dact = turn(
        sz, xb, rows_b, fourth, gain_one, gain_two, mix, up, act, down, g
    )
    sent, rows_a = lax.optimization_barrier((sent, rows_a))
    d_cols = sz.to_columns(sent)
    next_input = shift(tail(sz, xa, rows_a, fourth, gain_one, gain_two, mix, up, act, down), 1)
    grads = weight_grads(sz, factor, n1, dgate, n2, dup, dact, hs, g)
    d_out, spectrum_grad = middle_back(sz, d_cols, wide, kernel_here, mixed_b)
    d_rows = sz.to_rows(d_out)
    grads, d_rows = lax.optimization_barrier((grads, d_rows))
    upstream = shift(last(sz, xb, d_rows, first, gain_one, mix, dgate, dy), -1)
    grads = lax.psum_scatter(grads, "seq", scatter_dimension=0, tiled=True)
    w, u = width // NB, up.shape[1]
    down_grad = jnp.concatenate(
        [grads[:, w + 2 * u + k * w : w + 2 * u + (k + 1) * w] for k in range(u // w)], axis=0
    )
    return (
        next_input[None],
        upstream[None],
        spectrum_grad.reshape(spectrum.shape),
        grads[None, :, :w],
        grads[None, :, w : w + u],
        grads[None, :, w + u : w + 2 * u],
        down_grad[None],
    )


def solution(mesh):
    in_specs = (
        P("section", "seq", None),
        P("section", "seq", None),
        P("section", "seq", None),
        P("section", None),
        P("section", None),
        P("section", "seq", None, None),
        P("section", "seq", None, None),
        P("section", None, "seq", None),
        P("section", "seq", None, None),
        P("section", "seq", None, None),
        P("section", None, None),
        P("section", None, None),
        P("section", None, None),
        P("section", None, None),
    )
    out_specs = (
        P("section", "seq", None),
        P("section", "seq", None),
        P("section", None, "seq", None),
        P("section", "seq", None),
        P("section", "seq", None),
        P("section", "seq", None),
        P("section", "seq", None),
    )
    return jax.shard_map(shards, mesh=mesh, in_specs=in_specs, out_specs=out_specs, check_vma=False)
```

time: 416 us -> 301 us (0.72); the launches traced: 410 us -> 299 us
  matrix products: 96.6 us -> 0 us
  Pallas kernels: 0 us -> 73.6 us
  local copies, waits for them, and re-layouts: 124 us -> 54.7 us
  other arithmetic: 51.3 us -> 0.94 us
  blocking collectives: 0 us -> 30.4 us
  waiting for transfers between devices: 88 us -> 97.2 us
  starting transfers between devices: 34.7 us -> 27.9 us
    dot_general x26 -> x0, matrix products: 96.6 us -> none  [the longest x7 43.8 us: block_apply(): jnp.einsum('ynq,nqd->ynd', value_array.reshape(item_count, block_list, -1...]
    pallas_call x0 -> x10, Pallas kernels: none -> 73.6 us  [the longest x2 20.3 us: middle(): pl.pallas_call(middle_kernel, grid=(sz.width // part,), in_specs=[strip,...]
    convert_element_type x9 -> x0, local copies, waits for them, and re-layouts: 33.2 us -> none  [the longest x2 8.44 us: mixer_front(): return (scale, normed, folded.astype(jnp.bfloat16))]
    reshape x6 -> x0, local copies, waits for them, and re-layouts: 31.3 us -> none  [the longest x3 16.5 us: block_apply(): return final_output.reshape(item_count, -1)]
    all_to_all x0 -> x1, blocking collectives: none -> 30.4 us  [to_columns(): lax.all_to_all(array, 'seq', split_axis=0, concat_axis=0, tiled=True)]
    unnamed x97 -> x86, local copies, waits for them, and re-layouts: 25 us -> 50.7 us
    all_to_all x6 -> x5, waiting for transfers between devices: 33.1 us -> 52.5 us  [the longest x2 27.9 us: to_columns(): lax.all_to_all(array, 'seq', split_axis=0, concat_axis=0, tiled=True)]
    transpose x2 -> x0, other arithmetic: 17.2 us -> none  [shuffle(): return value_array.reshape(item_count, block_list, block_list, -1).transp...]
  transfers between devices with their start and end apart: 12 -> 8, of which waited for: 7 -> 7; matrix products, arithmetic and copies ran while one was open for 45% -> 0% of each run, Pallas kernels for 0% -> 20%
where the time goes in v1:
time: 301 us; the launch traced here: 299 us
  waiting for transfers between devices  97.2 us (32%)
  Pallas kernels  73.6 us (24%)
  local copies, waits for them, and re-layouts  54.7 us (18%)
  blocking collectives  30.4 us (10%)
  starting transfers between devices  27.9 us (9%)
  between operations  14.4 us (5%)
    unnamed x86, local copies, waits for them, and re-layouts  50.7 us
    ppermute x2, waiting for transfers between devices, shift(): return lax.ppermute(array, 'section', pairs)  44.7 us
    all_to_all x1, blocking collectives, to_columns(): lax.all_to_all(array, 'seq', split_axis=0, concat_axis=0, tiled=True)  30.4 us
    all_to_all x2, waiting for transfers between devices, to_columns(): lax.all_to_all(array, 'seq', split_axis=0, concat_axis=0, tiled=True)  27.9 us
    all_to_all x3, waiting for transfers between devices, to_rows(): lax.all_to_all(array, 'seq', split_axis=0, concat_axis=0, tiled=True)  24.6 us
    pallas_call x2, Pallas kernels, middle(): pl.pallas_call(middle_kernel, grid=(sz.width // part,), in_specs=[strip,...  20.3 us
    pallas_call x1, Pallas kernels, turn(): pl.pallas_call(functools.partial(turn_kernel, sz), grid=(sz.rows // sz.pe...  16.9 us
    all_to_all x3, starting transfers between devices, to_rows(): lax.all_to_all(array, 'seq', split_axis=0, concat_axis=0, tiled=True)  13.3 us
  transfers between devices with their start and end apart: 8, of which 7 were waited for; matrix products, arithmetic and copies ran while one was open for 0% of the time, Pallas kernels for 20%

profile of v1, /device:TPU:0, one launch (start us, length us, event | category | flops | bytes accessed | tf_op | source)
XLA Modules:
  0.0 299.1 jit_solution(562239790525261554)
XLA Ops:
  7.2 1.6 copy-done.5
  8.8 0.9 copy-done.17
  9.7 0.7 copy-done.29
  10.4 1.8 front.3
  12.2 1.3 copy-done.11
  13.5 5.3 %all-to-all-start = ((bf16[8,8,16,1024]{3,2,1,0:T(8,128)(2,1)}), bf16[8,8,16,1024]{3,2,1,0:T(8,128)(2,1)S(1)}, u32[]{:S(2)}, u32[]{:S(2)}) async-start(bf16[8,8,16,1024]{3,2,1,0:T(8,128)(2,1)} %copy-done.11), calls=%async_computation | async-start | bytes 4194304 | tf_op jit(solution)/shard_map/all_to_all | solution.py:93
  18.8 1.6 copy-done.23
  20.4 1.8 front.2
  22.2 1.3 copy-done.10
  23.5 21.9 %all-to-all-done = bf16[8,8,16,1024]{3,2,1,0:T(8,128)(2,1)S(1)} async-done(((bf16[8,8,16,1024]{3,2,1,0:T(8,128)(2,1)}), bf16[8,8,16,1024]{3,2,1,0:T(8,128)(2,1)S(1)}, u32[]{:S(2)}, u32[]{:S(2)}) %all-to-all-start) | async-done | bytes 2097184 | tf_op jit(solution)/shard_map/all_to_all | solution.py:93
  45.5 1.3 copy-done.8
  46.8 4.3 %all-to-all-start.1 = ((bf16[8,8,16,1024]{3,2,1,0:T(8,128)(2,1)}), bf16[8,8,16,1024]{3,2,1,0:T(8,128)(2,1)}, u32[]{:S(2)}, u32[]{:S(2)}) async-start(bf16[8,8,16,1024]{3,2,1,0:T(8,128)(2,1)} %copy-done.10), calls=%async_computation.1 | async-start | bytes 4194304 | tf_op jit(solution)/shard_map/all_to_all | solution.py:93
  51.1 0.3 copy.24
  51.4 0.3 copy.23
  51.7 0.2 copy.22
  51.9 0.2 copy.21
  52.0 0.3 pad_maximum_fusion.thin_ref
  52.3 2.8 expand.1.second_ref.third_ref
  55.2 10.0 %middle.2 = (bf16[1024,1024]{1,0:T(8,128)(2,1)S(1)}, f32[1024,1024]{1,0:T(8,128)S(1)}) custom-call(bf16[1024,1024]{1,0:T(8,128)(2,1)S(1)} %bitcast.47, bf16[4,1024,1024]{2,1,0:T(8,128)(2,1)S(1)} %expand.1.second_ref.third_ref, bf16[4,1024,1024]{2,1,0:T(8,128)(2,1)S(1)} %expand.1.second_ref.third_ref, bf16[1024,1024]{1,0:T(8,128)(2,1)S(1)} %bitcast.41), custom_call_target="tpu_custom_call" | custom-call | flops 4294967296 | bytes 10485760 | tf_op jit(solution)/shard_map/middle/pallas_call | solution.py:181
  65.2 3.3 %copy-done = bf16[4,1024,1024]{2,1,0:T(8,128)(2,1)} copy-done((bf16[4,1024,1024]{2,1,0:T(8,128)(2,1)}, bf16[4,1024,1024]{2,1,0:T(8,128)(2,1)S(1)}, u32[]{:S(2)}) %copy-start) | copy-done | bytes 8388632
  68.5 2.1 copy-done.13
  70.5 1.3 copy-done.26
  71.9 5.9 %all-to-all-done.1 = bf16[8,8,16,1024]{3,2,1,0:T(8,128)(2,1)} async-done(((bf16[8,8,16,1024]{3,2,1,0:T(8,128)(2,1)}), bf16[8,8,16,1024]{3,2,1,0:T(8,128)(2,1)}, u32[]{:S(2)}, u32[]{:S(2)}) %all-to-all-start.1) | async-done | bytes 2097184 | tf_op jit(solution)/shard_map/all_to_all | solution.py:93
  77.8 4.3 %all-to-all-start.2 = ((bf16[8,8,16,1024]{3,2,1,0:T(8,128)(2,1)}), bf16[8,8,16,1024]{3,2,1,0:T(8,128)(2,1)}, u32[]{:S(2)}, u32[]{:S(2)}) async-start(bf16[8,8,16,1024]{3,2,1,0:T(8,128)(2,1)} %bitcast.58), calls=%async_computation.2 | async-start | bytes 4194304 | tf_op jit(solution)/shard_map/all_to_all | solution.py:98
  82.1 3.4 %copy-done.1 = bf16[4,1024,1024]{2,1,0:T(8,128)(2,1)S(1)} copy-done((bf16[4,1024,1024]{2,1,0:T(8,128)(2,1)S(1)}, bf16[4,1024,1024]{2,1,0:T(8,128)(2,1)}, u32[]{:S(2)}) %copy-start.1) | copy-done | bytes 8388632
  85.5 10.3 %middle.3 = bf16[1024,1024]{1,0:T(8,128)(2,1)S(1)} custom-call(bf16[1024,1024]{1,0:T(8,128)(2,1)} %bitcast.15.x_ref, bf16[4,1024,1024]{2,1,0:T(8,128)(2,1)S(1)} %copy-done.1, bf16[4,1024,1024]{2,1,0:T(8,128)(2,1)S(1)} %copy-done.1, bf16[1024,1024]{1,0:T(8,128)(2,1)S(1)} %bitcast.42), custom_call_target="tpu_custom_call" | custom-call | flops 4294967296 | bytes 10485760 | tf_op jit(solution)/shard_map/middle/pallas_call | solution.py:181
  95.8 1.3 copy-done.12
  97.1 11.7 %all-to-all-done.2.b1_ref = bf16[8,8,16,1024]{3,2,1,0:T(8,128)(2,1)} async-done(((bf16[8,8,16,1024]{3,2,1,0:T(8,128)(2,1)}), bf16[8,8,16,1024]{3,2,1,0:T(8,128)(2,1)}, u32[]{:S(2)}, u32[]{:S(2)}) %all-to-all-start.2) | async-done | bytes 2097184 | tf_op jit(solution)/shard_map/all_to_all | solution.py:98
  108.8 4.5 %all-to-all-start.3 = ((bf16[8,8,16,1024]{3,2,1,0:T(8,128)(2,1)}), bf16[8,8,16,1024]{3,2,1,0:T(8,128)(2,1)}, u32[]{:S(2)}, u32[]{:S(2)}) async-start(bf16[8,8,16,1024]{3,2,1,0:T(8,128)(2,1)} %bitcast.49), calls=%async_computation.3 | async-start | bytes 4194304 | tf_op jit(solution)/shard_map/all_to_all | solution.py:98
  113.3 1.2 copy-done.31
  114.6 1.2 copy-done.33
  115.8 1.2 copy-done.35
  117.0 16.9 %turn.1 = (bf16[8,8,16,1024]{3,2,1,0:T(8,128)(2,1)S(1)}, bf16[1024,1024]{1,0:T(8,128)(2,1)}, bf16[1024,1024]{1,0:T(8,128)(2,1)}, bf16[1024,1024]{1,0:T(8,128)(2,...) custom-call(bf16[1024,1024]{1,0:T(8,128)(2,1)} %bitcast.44, ...), custom_call_target="tpu_custom_call" | custom-call | flops 8589934592 | bytes 31457280 | tf_op jit(solution)/shard_map/turn/pallas_call | solution.py:369
  134.0 1.3 copy-done.27
  135.3 4.7 %all-to-all-done.3.b1_ref = bf16[8,8,16,1024]{3,2,1,0:T(8,128)(2,1)} async-done(((bf16[8,8,16,1024]{3,2,1,0:T(8,128)(2,1)}), bf16[8,8,16,1024]{3,2,1,0:T(8,128)(2,1)}, u32[]{:S(2)}, u32[]{:S(2)}) %all-to-all-start.3) | async-done | bytes 2097184 | tf_op jit(solution)/shard_map/all_to_all | solution.py:98
  139.9 30.4 %all_to_all.30 = bf16[8,8,16,1024]{3,2,1,0:T(8,128)(2,1)S(1)} all-to-all(bf16[8,8,16,1024]{3,2,1,0:T(8,128)(2,1)} %copy-done.27), channel_id=1, replica_groups=mesh['section'=4,'seq'=8] {'seq'}, dimensions={0} | all-to-all | bytes 4194304 | tf_op jit(solution)/shard_map/all_to_all | solution.py:93
  170.3 3.4 %copy-done.2 = bf16[4,1024,1024]{2,1,0:T(8,128)(2,1)S(1)} copy-done((bf16[4,1024,1024]{2,1,0:T(8,128)(2,1)S(1)}, bf16[4,1024,1024]{2,1,0:T(8,128)(2,1)}, u32[]{:S(2)}) %copy-start.2) | copy-done | bytes 8388632
  173.7 10.8 %middle_back.1 = (bf16[1024,1024]{1,0:T(8,128)(2,1)S(1)}, bf16[1024,1024]{1,0:T(8,128)(2,1)}) custom-call(bf16[1024,1024]{1,0:T(8,128)(2,1)S(1)} %bitcast.48, bf16[4,1024,1024]{2,1,0:T(8,128)(2,1)S(1)} %copy-done.2, bf16[4,1024,1024]{2,1,0:T(8,128)(2,1)S(1)} %copy-done.2, bf16[1024,1024]{1,0:T(8,128)(2,1)S(1)} %bitcast.43, f32[1024,1024]{1,0:T(8,128)S(1)} %copy-done.14), custom_call_target="tpu_custom_call" | custom-call | flops 4294967296 | bytes 12582912 | tf_op jit(solution)/shard_map/middle_back/pallas_call | solution.py:211
  184.5 1.3 copy-done.25
  185.8 4.5 %all-to-all-start.5 = ((bf16[8,8,16,1024]{3,2,1,0:T(8,128)(2,1)}), bf16[8,8,16,1024]{3,2,1,0:T(8,128)(2,1)}, u32[]{:S(2)}, u32[]{:S(2)}) async-start(bf16[8,8,16,1024]{3,2,1,0:T(8,128)(2,1)} %bitcast.57), calls=%async_computation.5 | async-start | bytes 4194304 | tf_op jit(solution)/shard_map/all_to_all | solution.py:98
  190.3 0.2 reduce-scatter.2.cloned.1.call-start
  190.5 2.2 copy-done.15
  192.7 2.2 copy-done.16
  194.9 1.6 copy-done.19
  196.5 1.6 copy-done.21
  198.1 1.6 copy-done.22
  199.7 7.2 %weight_grads.1 = bf16[1024,1792]{1,0:T(8,128)(2,1)S(1)} custom-call(bf16[1024,1024]{1,0:T(8,128)(2,1)S(1)} %copy-done.21, bf16[1024,1024]{1,0:T(8,128)(2,1)S(1)} %copy-done.7, bf16[1024,1024]{1,0:T(8,128)(2,1)S(1)} %copy-done.22, bf16[1024,2048]{1,0:T(8,128)(2,1)S(1)} %copy-done.15, bf16[1024,2048]{1,0:T(8,128)(2,1)S(1)} %copy-done.16, ...), custom_call_target="tpu_custom_call" | custom-call | flops 3758096384 | bytes 25165824 | tf_op jit(solution)/shard_map/weight_grads/pallas_call | solution.py:403
  206.9 1.8 copy-done.4
  208.7 8.3 %all-to-all-done.5.d_ref = bf16[8,8,16,1024]{3,2,1,0:T(8,128)(2,1)} async-done(((bf16[8,8,16,1024]{3,2,1,0:T(8,128)(2,1)}), bf16[8,8,16,1024]{3,2,1,0:T(8,128)(2,1)}, u32[]{:S(2)}, u32[]{:S(2)}) %all-to-all-start.5) | async-done | bytes 2097184 | tf_op jit(solution)/shard_map/all_to_all | solution.py:98
  217.0 1.6 copy-done.24
  218.6 1.2 copy-done.32
  219.8 1.2 copy-done.34
  221.0 1.5 copy-done.36
  222.5 7.4 %tail.1 = bf16[1024,1024]{1,0:T(8,128)(2,1)S(1)} custom-call(bf16[1024,1024]{1,0:T(8,128)(2,1)S(1)} %bitcast.56, bf16[8,8,16,1024]{3,2,1,0:T(8,128)(2,1)} %all-to-all-done.3.b1_ref, bf16[8,128,128]{2,1,0:T(8,128)(2,1)S(1)} %bitcast.69, f32[1,1024]{1,0:T(1,128)S(1)} %copy-done.30, f32[1,1024]{1,0:T(1,128)S(1)} %copy-done.38, bf16[1024,256]{1,0:T(8,128)(2,1)S(1)} %bitcast.60, ...), custom_call_target="tpu_custom_call" | custom-call | flops 4294967296 | bytes 8388608 | tf_op jit(solution)/shard_map/tail/pallas_call | solution.py:289
  229.9 3.4 %collective-permute-start = (bf16[1024,1024]{1,0:T(8,128)(2,1)S(1)}, bf16[1024,1024]{1,0:T(8,128)(2,1)S(1)}, u32[]{:S(2)}, u32[]{:S(2)}) collective-permute-start(bf16[1024,1024]{1,0:T(8,128)(2,1)S(1)} %tail.1), channel_id=1, source_target_pairs={{0,8},{8,16},{16,24},{1,9},{9,17},{17,25},{2,10},{10,18},{18,26},{... | collective-permute-start | bytes 6291464 | tf_op jit(solution)/shard_map/ppermute | solution.py:461
  233.4 4.6 %last.1 = bf16[1024,1024]{1,0:T(8,128)(2,1)S(1)} custom-call(bf16[1024,1024]{1,0:T(8,128)(2,1)S(1)} %bitcast.46, bf16[8,8,16,1024]{3,2,1,0:T(8,128)(2,1)} %all-to-all-done.5.d_ref, bf16[8,128,128]{2,1,0:T(8,128)(2,1)S(1)} %bitcast.52, f32[1,1024]{1,0:T(1,128)S(1)} %copy-done.30, bf16[1024,256]{1,0:T(8,128)(2,1)S(1)} %bitcast.61, ...), custom_call_target="tpu_custom_call" | custom-call | flops 805306368 | bytes 10485760 | tf_op jit(solution)/shard_map/last/pallas_call | solution.py:438
  238.0 1.3 collective-permute-start.1
  239.3 35.7 %collective-permute-done = bf16[1024,1024]{1,0:T(8,128)(2,1)S(1)} collective-permute-done((bf16[1024,1024]{1,0:T(8,128)(2,1)S(1)}, bf16[1024,1024]{1,0:T(8,128)(2,1)S(1)}, u32[]{:S(2)}, u32[]{:S(2)}) %collective-permute-start) | collective-permute-done | bytes 2097184 | tf_op jit(solution)/shard_map/ppermute | solution.py:461
  275.1 8.9 %collective-permute-done.1 = bf16[1024,1024]{1,0:T(8,128)(2,1)S(1)} collective-permute-done((bf16[1024,1024]{1,0:T(8,128)(2,1)S(1)}, bf16[1024,1024]{1,0:T(8,128)(2,1)S(1)}, u32[]{:S(2)}, u32[]{:S(2)}) %collective-permute-start.1) | collective-permute-done | bytes 2097184 | tf_op jit(solution)/shard_map/ppermute | solution.py:461
  284.0 1.5 fusion
  285.5 0.7 maximum_bitcast_fusion
  286.2 1.7 slice_bitcast_fusion
  287.9 3.1 %copy.27 = bf16[1,1024,1024]{2,1,0:T(8,128)(2,1)} copy(bf16[1,1024,1024]{2,1,0:T(8,128)(2,1)} %bitcast.70) | data formatting | bytes 4194304
  291.0 1.3 copy.28
  (58 shorter events, 0.1 us)
Async XLA Ops:
  7.2 1.6 copy-start.5
  8.8 0.9 copy-start.17
  9.7 0.7 copy-start.29
  12.2 1.3 copy-start.11
  13.5 5.3 %copy-start.18 = (bf16[1,8,128,128]{3,2,1,0:T(8,128)(2,1)S(1)}, bf16[1,8,128,128]{3,2,1,0:T(8,128)(2,1)}, u32[]{:S(2)}) copy-start(bf16[1,8,128,128]{3,2,1,0:T(8,128)(2,1)} %param.19) | copy-start | bytes 786436
  13.5 5.3 %copy-start.30 = (f32[1,1024]{1,0:T(1,128)S(1)}, f32[1,1024]{1,0:T(1,128)}, u32[]{:S(2)}) copy-start(f32[1,1024]{1,0:T(1,128)} %gain_ref.5) | copy-start | bytes 12292
  13.5 31.9 %all-to-all-start = ((bf16[8,8,16,1024]{3,2,1,0:T(8,128)(2,1)}), bf16[8,8,16,1024]{3,2,1,0:T(8,128)(2,1)S(1)}, u32[]{:S(2)}, u32[]{:S(2)}) async-start(bf16[8,8,16,1024]{3,2,1,0:T(8,128)(2,1)} %copy-done.11), calls=%async_computation | async-start | bytes 4194304 | tf_op jit(solution)/shard_map/all_to_all | solution.py:93
  18.8 1.6 copy-start.23
  22.2 1.3 copy-start.10
  45.5 1.3 copy-start.8
  45.5 5.7 %copy-start.41 = (bf16[1,16,64,64]{3,2,1,0:T(8,128)(2,1)S(1)}, bf16[1,16,64,64]{3,2,1,0:T(8,128)(2,1)}, u32[]{:S(2)}) copy-start(bf16[1,16,64,64]{3,2,1,0:T(8,128)(2,1)} %param.20) | copy-start | bytes 393220
  45.5 5.9 %copy-start.40 = (bf16[1,16,64,64]{3,2,1,0:T(8,128)(2,1)S(1)}, bf16[1,16,64,64]{3,2,1,0:T(8,128)(2,1)}, u32[]{:S(2)}) copy-start(bf16[1,16,64,64]{3,2,1,0:T(8,128)(2,1)} %param.22) | copy-start | bytes 393220
  46.8 31.0 %all-to-all-start.1 = ((bf16[8,8,16,1024]{3,2,1,0:T(8,128)(2,1)}), bf16[8,8,16,1024]{3,2,1,0:T(8,128)(2,1)}, u32[]{:S(2)}, u32[]{:S(2)}) async-start(bf16[8,8,16,1024]{3,2,1,0:T(8,128)(2,1)} %copy-done.10), calls=%async_computation.1 | async-start | bytes 4194304 | tf_op jit(solution)/shard_map/all_to_all | solution.py:93
  52.3 2.8 copy-start.3
  52.3 2.8 copy-start.9
  65.2 3.3 %copy-start = (bf16[4,1024,1024]{2,1,0:T(8,128)(2,1)}, bf16[4,1024,1024]{2,1,0:T(8,128)(2,1)S(1)}, u32[]{:S(2)}) copy-start(bf16[4,1024,1024]{2,1,0:T(8,128)(2,1)S(1)} %expand.1.second_ref.third_ref) | copy-start | bytes 25165828
  68.5 2.1 copy-start.13
  70.5 1.3 copy-start.26
  77.8 31.0 %all-to-all-start.2 = ((bf16[8,8,16,1024]{3,2,1,0:T(8,128)(2,1)}), bf16[8,8,16,1024]{3,2,1,0:T(8,128)(2,1)}, u32[]{:S(2)}, u32[]{:S(2)}) async-start(bf16[8,8,16,1024]{3,2,1,0:T(8,128)(2,1)} %bitcast.58), calls=%async_computation.2 | async-start | bytes 4194304 | tf_op jit(solution)/shard_map/all_to_all | solution.py:98
  82.1 3.4 %copy-start.1 = (bf16[4,1024,1024]{2,1,0:T(8,128)(2,1)S(1)}, bf16[4,1024,1024]{2,1,0:T(8,128)(2,1)}, u32[]{:S(2)}) copy-start(bf16[4,1024,1024]{2,1,0:T(8,128)(2,1)} %copy-done) | copy-start | bytes 25165828
  95.8 1.3 copy-start.12
  108.8 4.5 %copy-start.28 = (bf16[1,1024,256]{2,1,0:T(8,128)(2,1)S(1)}, bf16[1,1024,256]{2,1,0:T(8,128)(2,1)}, u32[]{:S(2)}) copy-start(bf16[1,1024,256]{2,1,0:T(8,128)(2,1)} %param.24) | copy-start | bytes 1572868
  108.8 4.5 %copy-start.37 = (bf16[1,8,128,128]{3,2,1,0:T(8,128)(2,1)S(1)}, bf16[1,8,128,128]{3,2,1,0:T(8,128)(2,1)}, u32[]{:S(2)}) copy-start(bf16[1,8,128,128]{3,2,1,0:T(8,128)(2,1)} %param.23) | copy-start | bytes 786436
  108.8 4.5 %copy-start.38 = (f32[1,1024]{1,0:T(1,128)S(1)}, f32[1,1024]{1,0:T(1,128)}, u32[]{:S(2)}) copy-start(f32[1,1024]{1,0:T(1,128)} %gain_two_ref.3) | copy-start | bytes 12292
  108.8 31.1 %all-to-all-start.3 = ((bf16[8,8,16,1024]{3,2,1,0:T(8,128)(2,1)}), bf16[8,8,16,1024]{3,2,1,0:T(8,128)(2,1)}, u32[]{:S(2)}, u32[]{:S(2)}) async-start(bf16[8,8,16,1024]{3,2,1,0:T(8,128)(2,1)} %bitcast.49), calls=%async_computation.3 | async-start | bytes 4194304 | tf_op jit(solution)/shard_map/all_to_all | solution.py:98
  113.3 1.2 copy-start.31
  114.5 1.2 copy-start.33
  115.8 1.2 copy-start.35
  133.9 1.3 copy-start.27
  139.9 30.4 %copy-start.14 = (f32[1024,1024]{1,0:T(8,128)S(1)}, f32[1024,1024]{1,0:T(8,128)}, u32[]{:S(2)}) copy-start(f32[1024,1024]{1,0:T(8,128)} %copy-done.13) | copy-start | bytes 12582916
  170.3 3.4 %copy-start.2 = (bf16[4,1024,1024]{2,1,0:T(8,128)(2,1)S(1)}, bf16[4,1024,1024]{2,1,0:T(8,128)(2,1)}, u32[]{:S(2)}) copy-start(bf16[4,1024,1024]{2,1,0:T(8,128)(2,1)} %copy-done) | copy-start | bytes 25165828
  184.5 1.3 copy-start.25
  185.8 4.7 %copy-start.7 = (bf16[1024,1024]{1,0:T(8,128)(2,1)S(1)}, bf16[1024,1024]{1,0:T(8,128)(2,1)}, u32[]{:S(2)}) copy-start(bf16[1024,1024]{1,0:T(8,128)(2,1)} %get-tuple-element.39.dgate.dgate_ref) | copy-start | bytes 6291460
  185.8 31.1 %all-to-all-start.5 = ((bf16[8,8,16,1024]{3,2,1,0:T(8,128)(2,1)}), bf16[8,8,16,1024]{3,2,1,0:T(8,128)(2,1)}, u32[]{:S(2)}, u32[]{:S(2)}) async-start(bf16[8,8,16,1024]{3,2,1,0:T(8,128)(2,1)} %bitcast.57), calls=%async_computation.5 | async-start | bytes 4194304 | tf_op jit(solution)/shard_map/all_to_all | solution.py:98
  190.3 93.7 %reduce-scatter.2.cloned.1.call-start = ((), (), s32[]{:S(2)}) async-start(), calls=%async_computation.7 | async-start | bytes 4128768 | tf_op jit(solution)/shard_map/reduce_scatter | solution.py:517
  190.5 2.2 copy-start.15
  192.7 2.2 copy-start.16
  194.9 1.6 copy-start.19
  196.5 1.6 copy-start.21
  198.1 1.6 copy-start.22
  206.9 1.8 copy-start.4
  217.0 1.6 copy-start.24
  218.6 1.2 copy-start.32
  219.8 1.2 copy-start.34
  221.0 1.5 copy-start.36
  222.5 10.9 %copy-start.6 = (bf16[1,1024,1024]{2,1,0:T(8,128)(2,1)S(1)}, bf16[1,1024,1024]{2,1,0:T(8,128)(2,1)}, u32[]{:S(2)}) copy-start(bf16[1,1024,1024]{2,1,0:T(8,128)(2,1)} %param.15) | copy-start | bytes 6291460
  222.5 10.9 %copy-start.20 = (bf16[1024,1024]{1,0:T(8,128)(2,1)S(1)}, bf16[1024,1024]{1,0:T(8,128)(2,1)}, u32[]{:S(2)}) copy-start(bf16[1024,1024]{1,0:T(8,128)(2,1)} %get-tuple-element.48.dy_ref) | copy-start | bytes 6291460
  229.9 45.1 %collective-permute-start = (bf16[1024,1024]{1,0:T(8,128)(2,1)S(1)}, bf16[1024,1024]{1,0:T(8,128)(2,1)S(1)}, u32[]{:S(2)}, u32[]{:S(2)}) collective-permute-start(bf16[1024,1024]{1,0:T(8,128)(2,1)S(1)} %tail.1), channel_id=1, source_target_pairs={{0,8},{8,16},{16,24},{1,9},{9,17},{17,25},{2,10},{10,18},{18,26},{... | collective-permute-start | bytes 6291464 | tf_op jit(solution)/shard_map/ppermute | solution.py:461
  238.0 46.0 %collective-permute-start.1 = (bf16[1024,1024]{1,0:T(8,128)(2,1)S(1)}, bf16[1024,1024]{1,0:T(8,128)(2,1)S(1)}, u32[]{:S(2)}, u32[]{:S(2)}) collective-permute-start(bf16[1024,1024]{1,0:T(8,128)(2,1)S(1)} %last.1), channel_id=1, source_target_pairs={{8,0},{16,8},{24,16},{9,1},{17,9},{25,17},{10,2},{18,10},{26,18},{... | collective-permute-start | bytes 6291464 | tf_op jit(solution)/shard_map/ppermute | solution.py:461
  275.1 8.9 %copy-start.39 = (bf16[1024,1024]{1,0:T(8,128)(2,1)}, bf16[1024,1024]{1,0:T(8,128)(2,1)S(1)}, u32[]{:S(2)}) copy-start(bf16[1024,1024]{1,0:T(8,128)(2,1)S(1)} %collective-permute-done) | copy-start | bytes 6291460
Sparse Core Ops, SparseCore 0:
  217.1 48.1 reduce-scatter.1

commit v2 on v1

--- a/solution.py
+++ b/solution.py
@@ -12,7 +12,7 @@
 EPS = 1e-06
 F32 = jnp.float32
 BF16 = jnp.bfloat16
-MIB = 1024 * 1024
+VMEM = 56 * 1024 * 1024
 
 
 def dot(a, b):
@@ -42,10 +42,93 @@
     return array[:, b * width : (b + 1) * width]
 
 
-def params(mib, steps=1):
-    return pltpu.CompilerParams(
-        dimension_semantics=("arbitrary",) * steps, vmem_limit_bytes=mib * MIB
-    )
+def call(body, grid, in_specs, out_specs, out_shape, price, name, *args):
+    return pl.pallas_call(
+        body,
+        grid=(grid,),
+        in_specs=in_specs,
+        out_specs=out_specs,
+        out_shape=out_shape,
+        compiler_params=pltpu.CompilerParams(
+            dimension_semantics=("arbitrary",), vmem_limit_bytes=VMEM
+        ),
+        cost_estimate=price,
+        name=name,
+    )(*args)
+
+
+def call_exchanging(
+    sz, send, span, cid, body, grid, in_specs, out_specs, out_shape, price, name, *args
+):
+    n = sz.n
+    count = len(in_specs)
+
+    def kernel(send_ref, *refs):
+        ins, recv_ref = refs[:count], refs[count]
+        outs = refs[count + 1 : -3]
+        send_sem, recv_sem, own_sem = refs[-3:]
+        step = pl.program_id(0)
+        me = lax.axis_index("seq")
+
+        def copies():
+            own = pltpu.make_async_copy(
+                send_ref.at[me, pl.ds(span[0], span[1])], recv_ref.at[me], own_sem
+            )
+            far = [
+                pltpu.make_async_remote_copy(
+                    src_ref=send_ref.at[lax.rem(me + k, n), pl.ds(span[0], span[1])],
+                    dst_ref=recv_ref.at[me],
+                    send_sem=send_sem.at[k - 1],
+                    recv_sem=recv_sem.at[k - 1],
+                    device_id={"seq": lax.rem(me + k, n)},
+                    device_id_type=pl.DeviceIdType.MESH,
+                )
+                for k in range(1, n)
+            ]
+            return far + [own]
+
+        @pl.when(step == 0)
+        def _():
+            barrier = pltpu.get_barrier_semaphore()
+            for k in range(1, n):
+                pl.semaphore_signal(
+                    barrier,
+                    inc=1,
+                    device_id={"seq": lax.rem(me + k, n)},
+                    device_id_type=pl.DeviceIdType.MESH,
+                )
+            pl.semaphore_wait(barrier, n - 1)
+            for copy in copies():
+                copy.start()
+
+        body(*ins, *outs)
+
+        @pl.when(step == grid - 1)
+        def _():
+            for copy in copies():
+                copy.wait()
+
+    shape = (n, span[1]) + send.shape[2:]
+    return pl.pallas_call(
+        kernel,
+        grid=(grid,),
+        in_specs=[pl.BlockSpec(memory_space=pl.ANY)] + in_specs,
+        out_specs=[pl.BlockSpec(memory_space=pl.ANY)] + out_specs,
+        out_shape=[jax.ShapeDtypeStruct(shape, send.dtype)] + out_shape,
+        scratch_shapes=[
+            pltpu.SemaphoreType.DMA((n - 1,)),
+            pltpu.SemaphoreType.DMA((n - 1,)),
+            pltpu.SemaphoreType.DMA(()),
+        ],
+        compiler_params=pltpu.CompilerParams(
+            dimension_semantics=("arbitrary",),
+            vmem_limit_bytes=VMEM,
+            collective_id=cid,
+            has_side_effects=True,
+        ),
+        cost_estimate=price,
+        name=name,
+    )(send, *args)
 
 
 def cost(flops, nbytes):
@@ -63,6 +146,7 @@
         self.tokens = rows * self.line
         self.per = 2 if rows % 2 == 0 else 1
         self.aligned = cols % 16 == 0
+        self.groups = cols // 8 if cols % 8 == 0 else 1
 
     def sent_shape(self):
         if self.aligned:
@@ -87,24 +171,27 @@
             return ref[:, r].reshape(self.line, self.width)
         return ref[r]
 
-    def to_columns(self, array):
-        if not self.aligned:
-            array = array.reshape(self.rows, self.n, self.cols, self.width).transpose(1, 0, 2, 3)
-        array = lax.all_to_all(array, "seq", split_axis=0, concat_axis=0, tiled=True)
+    def to_send(self, array):
+        if self.aligned:
+            return array
+        return array.reshape(self.rows, self.n, self.cols, self.width).transpose(1, 0, 2, 3)
+
+    def to_flat(self, array):
         return array.reshape(self.tall * self.cols, self.width)
 
+    def from_flat(self, array):
+        return array.reshape(self.n, self.rows, self.cols, self.width)
+
     def to_rows(self, array):
-        array = array.reshape(self.n, self.rows, self.cols, self.width)
-        array = lax.all_to_all(array, "seq", split_axis=0, concat_axis=0, tiled=True)
-        if not self.aligned:
-            array = array.transpose(1, 0, 2, 3).reshape(self.rows, self.line, self.width)
-        return array
-
-    def token_spec(self, width):
-        return pl.BlockSpec((self.per * self.line, width), lambda i: (i, 0))
-
-    def factor_spec(self):
-        return pl.BlockSpec((self.per, self.line, self.line), lambda i: (i, 0, 0))
+        if self.aligned:
+            return array
+        return array.transpose(1, 0, 2, 3).reshape(-1, self.line, self.width)
+
+    def token_spec(self, width, skip=0):
+        return pl.BlockSpec((self.per * self.line, width), lambda i: (i + skip, 0))
+
+    def factor_spec(self, skip=0):
+        return pl.BlockSpec((self.per, self.line, self.line), lambda i: (i + skip, 0, 0))
 
 
 def whole(shape):
@@ -118,112 +205,130 @@
         sz.put(sent_ref, r, dot(first_ref[r], normed).astype(BF16))
 
 
-def front(sz, x, gain, first):
-    return pl.pallas_call(
+def front_parts(sz, x, gain, first):
+    return (
         functools.partial(front_kernel, sz),
-        grid=(sz.rows // sz.per,),
-        in_specs=[sz.token_spec(sz.width), whole((1, sz.width)), sz.factor_spec()],
-        out_specs=sz.sent_spec(),
-        out_shape=jax.ShapeDtypeStruct(sz.sent_shape(), BF16),
-        compiler_params=params(16),
-        cost_estimate=cost(2 * sz.tokens * sz.line * sz.width, 4 * sz.tokens * sz.width),
-        name="front",
-    )(x, gain, first)
+        sz.rows // sz.per,
+        [sz.token_spec(sz.width), whole((1, sz.width)), sz.factor_spec()],
+        [sz.sent_spec()],
+        [jax.ShapeDtypeStruct(sz.sent_shape(), BF16)],
+        cost(2 * sz.tokens * sz.line * sz.width, 4 * sz.tokens * sz.width),
+        "front",
+        x,
+        gain,
+        first,
+    )
 
 
 def expand_kernel(cols, tall, thin_ref, wide_ref):
     size = tall * cols
     pick = lax.broadcasted_iota(jnp.int32, (tall, size), 1) // cols
     pick = (pick == lax.broadcasted_iota(jnp.int32, (tall, size), 0)).astype(F32).astype(BF16)
-    spread = dot(thin_ref[0], pick)
     left = lax.broadcasted_iota(jnp.int32, (size, size), 0) % cols
     right = lax.broadcasted_iota(jnp.int32, (size, size), 1) % cols
-    wide_ref[0] = jnp.where(left == right, spread, 0.0).astype(BF16)
+    for g in range(thin_ref.shape[1]):
+        spread = dot(thin_ref[0, g], pick)
+        wide_ref[0, g] = jnp.where(left == right, spread, 0.0).astype(BF16)
 
 
 def expand(sz, second, third):
-    size = sz.tall * sz.cols
-    thin = jnp.stack(
-        [
-            second.transpose(1, 0, 2).reshape(size, sz.tall),
-            third.transpose(1, 0, 2).reshape(size, sz.tall),
-            third.transpose(2, 0, 1).reshape(size, sz.tall),
-            second.transpose(2, 0, 1).reshape(size, sz.tall),
-        ]
-    )
-    return pl.pallas_call(
-        functools.partial(expand_kernel, sz.cols, sz.tall),
-        grid=(4,),
-        in_specs=[pl.BlockSpec((1, size, sz.tall), lambda i: (i, 0, 0))],
-        out_specs=pl.BlockSpec((1, size, size), lambda i: (i, 0, 0)),
-        out_shape=jax.ShapeDtypeStruct((4, size, size), BF16),
-        compiler_params=params(32),
-        cost_estimate=cost(8 * size * size * sz.tall, 8 * size * size),
-        name="expand",
-    )(thin)
-
-
-def middle_kernel(x_ref, second_ref, third_ref, spectrum_ref, out_ref, *mixed_ref):
-    mixed = dot(second_ref[0], x_ref[...])
+    inner = sz.cols // sz.groups
+    size = sz.tall * inner
+
+    def thin(factor, order):
+        grouped = factor.reshape(sz.groups, inner, sz.tall, sz.tall)
+        return grouped.transpose(order).reshape(sz.groups, size, sz.tall)
+
+    ahead, back = (0, 2, 1, 3), (0, 3, 1, 2)
+    stack = jnp.stack(
+        [thin(second, ahead), thin(third, ahead), thin(third, back), thin(second, back)]
+    )
+    return call(
+        functools.partial(expand_kernel, inner, sz.tall),
+        4,
+        [pl.BlockSpec((1, sz.groups, size, sz.tall), lambda i: (i, 0, 0, 0))],
+        pl.BlockSpec((1, sz.groups, size, size), lambda i: (i, 0, 0, 0)),
+        jax.ShapeDtypeStruct((4, sz.groups, size, size), BF16),
+        cost(8 * sz.groups * size * size * sz.tall, 8 * sz.groups * size * size),
+        "expand",
+        stack,
+    )
+
+
+def mix_rows(sz, wide_ref, x):
+    if sz.groups == 1:
+        return dot(wide_ref[0, 0], x.astype(BF16))
+    part = x.shape[1]
+    inner = sz.cols // sz.groups
+    x = x.reshape(sz.tall, sz.cols, part)
+    outs = []
+    for g in range(sz.groups):
+        piece = x[:, g * inner : (g + 1) * inner].reshape(sz.tall * inner, part).astype(BF16)
+        outs.append(dot(wide_ref[0, g], piece).reshape(sz.tall, inner, part))
+    return jnp.concatenate(outs, axis=1).reshape(sz.tall * sz.cols, part)
+
+
+def middle_kernel(sz, x_ref, second_ref, third_ref, spectrum_ref, out_ref, *mixed_ref):
+    mixed = mix_rows(sz, second_ref, x_ref[...].astype(F32))
     if mixed_ref:
         mixed_ref[0][...] = mixed
-    filtered = (mixed * spectrum_ref[...].astype(F32)).astype(BF16)
-    out_ref[...] = dot(third_ref[0], filtered).astype(BF16)
-
-
-def middle(sz, x, wide, spectrum, keep):
+    filtered = mixed * spectrum_ref[...].astype(F32)
+    out_ref[...] = mix_rows(sz, third_ref, filtered).astype(BF16)
+
+
+def wide_spec(wide, which):
+    return pl.BlockSpec((1,) + wide.shape[1:], lambda i: (which, 0, 0, 0))
+
+
+def middle_parts(sz, x, wide, spectrum, keep):
     size = sz.tall * sz.cols
     part = 256
     strip = pl.BlockSpec((size, part), lambda i: (0, i))
     shapes = [jax.ShapeDtypeStruct((size, sz.width), BF16)]
     if keep:
         shapes.append(jax.ShapeDtypeStruct((size, sz.width), F32))
-    return pl.pallas_call(
-        middle_kernel,
-        grid=(sz.width // part,),
-        in_specs=[
-            strip,
-            pl.BlockSpec((1, size, size), lambda i: (0, 0, 0)),
-            pl.BlockSpec((1, size, size), lambda i: (1, 0, 0)),
-            strip,
-        ],
-        out_specs=[strip] * len(shapes),
-        out_shape=shapes,
-        compiler_params=params(28),
-        cost_estimate=cost(4 * size * size * sz.width, 10 * size * sz.width),
-        name="middle",
-    )(x, wide, wide, spectrum)
+    return (
+        functools.partial(middle_kernel, sz),
+        sz.width // part,
+        [strip, wide_spec(wide, 0), wide_spec(wide, 1), strip],
+        [strip] * len(shapes),
+        shapes,
+        cost(4 * size * size * sz.width // sz.groups, 10 * size * sz.width),
+        "middle",
+        x,
+        wide,
+        wide,
+        spectrum,
+    )
 
 
 def middle_back_kernel(
-    d_ref, third_ref, second_ref, spectrum_ref, mixed_ref, out_ref, grad_ref
+    sz, d_ref, third_ref, second_ref, spectrum_ref, mixed_ref, out_ref, grad_ref
 ):
-    d_filtered = dot(third_ref[0], d_ref[...])
+    d_filtered = mix_rows(sz, third_ref, d_ref[...].astype(F32))
     grad_ref[...] = (d_filtered * mixed_ref[...]).astype(BF16)
-    d_mixed = (d_filtered * spectrum_ref[...].astype(F32)).astype(BF16)
-    out_ref[...] = dot(second_ref[0], d_mixed).astype(BF16)
+    d_mixed = d_filtered * spectrum_ref[...].astype(F32)
+    out_ref[...] = mix_rows(sz, second_ref, d_mixed).astype(BF16)
 
 
 def middle_back(sz, d, wide, spectrum, mixed):
     size = sz.tall * sz.cols
     part = 256
     strip = pl.BlockSpec((size, part), lambda i: (0, i))
-    return pl.pallas_call(
-        middle_back_kernel,
-        grid=(sz.width // part,),
-        in_specs=[
-            strip,
-            pl.BlockSpec((1, size, size), lambda i: (2, 0, 0)),
-            pl.BlockSpec((1, size, size), lambda i: (3, 0, 0)),
-            strip,
-            strip,
-        ],
-        out_specs=[strip, strip],
-        out_shape=[jax.ShapeDtypeStruct((size, sz.width), BF16)] * 2,
-        compiler_params=params(28),
-        cost_estimate=cost(4 * size * size * sz.width, 12 * size * sz.width),
-        name="middle_back",
-    )(d, wide, wide, spectrum, mixed)
+    return call(
+        functools.partial(middle_back_kernel, sz),
+        sz.width // part,
+        [strip, wide_spec(wide, 2), wide_spec(wide, 3), strip, strip],
+        [strip, strip],
+        [jax.ShapeDtypeStruct((size, sz.width), BF16)] * 2,
+        cost(4 * size * size * sz.width // sz.groups, 12 * size * sz.width),
+        "middle_back",
+        d,
+        wide,
+        wide,
+        spectrum,
+        mixed,
+    )
 
 
 def tail_front(sz, x_ref, b1_ref, fourth_ref, gain_one, mix_ref):
@@ -285,17 +390,22 @@
     ] + [whole(w.shape) for w in weights]
 
 
-def tail(sz, x, b1, fourth, gain_one, gain_two, *weights):
-    return pl.pallas_call(
+def tail_parts(sz, x, b1, fourth, gain_one, gain_two, *weights):
+    return (
         functools.partial(tail_kernel, sz),
-        grid=(sz.rows // sz.per,),
-        in_specs=tail_specs(sz, weights),
-        out_specs=sz.token_spec(sz.width),
-        out_shape=jax.ShapeDtypeStruct((sz.tokens, sz.width), BF16),
-        compiler_params=params(40),
-        cost_estimate=cost(8 * sz.tokens * sz.width * sz.width // 2, 8 * sz.tokens * sz.width),
-        name="tail",
-    )(x, b1, fourth, gain_one, gain_two, *weights)
+        sz.rows // sz.per,
+        tail_specs(sz, weights),
+        [sz.token_spec(sz.width)],
+        [jax.ShapeDtypeStruct((sz.tokens, sz.width), BF16)],
+        cost(4 * sz.tokens * sz.width * sz.width, 8 * sz.tokens * sz.width),
+        "tail",
+        x,
+        b1,
+        fourth,
+        gain_one,
+        gain_two,
+        *weights,
+    )
 
 
 def turn_kernel(
@@ -362,21 +472,27 @@
         sz.put(sent_ref, r, t_dot(fourth_ref[r], part).astype(BF16))
 
 
-def turn(sz, x, b1, fourth, gain_one, gain_two, mix, up, act, down, g):
+def turn_parts(sz, x, b1, fourth, gain_one, gain_two, mix, up, act, down, g):
     weights = (mix, up, act, down)
     units = NB * up.shape[1]
     widths = [sz.width] * 4 + [units] * 3
-    return pl.pallas_call(
+    return (
         functools.partial(turn_kernel, sz),
-        grid=(sz.rows // sz.per,),
-        in_specs=tail_specs(sz, weights) + [sz.token_spec(sz.width)],
-        out_specs=[sz.sent_spec()] + [sz.token_spec(w) for w in widths],
-        out_shape=[jax.ShapeDtypeStruct(sz.sent_shape(), BF16)]
+        sz.rows // sz.per,
+        tail_specs(sz, weights) + [sz.token_spec(sz.width)],
+        [sz.sent_spec()] + [sz.token_spec(w) for w in widths],
+        [jax.ShapeDtypeStruct(sz.sent_shape(), BF16)]
         + [jax.ShapeDtypeStruct((sz.tokens, w), BF16) for w in widths],
-        compiler_params=params(48),
-        cost_estimate=cost(8 * sz.tokens * sz.width * sz.width, 30 * sz.tokens * sz.width),
-        name="turn",
-    )(x, b1, fourth, gain_one, gain_two, *weights, g)
+        cost(8 * sz.tokens * sz.width * sz.width, 30 * sz.tokens * sz.width),
+        "turn",
+        x,
+        b1,
+        fourth,
+        gain_one,
+        gain_two,
+        *weights,
+        g,
+    )
 
 
 def weights_kernel(factor, share, n1, dgate, n2, dup, dact, hs, g, out_ref):
@@ -394,22 +510,28 @@
         ]
 
 
-def weight_grads(sz, factor, n1, dgate, n2, dup, dact, hs, g):
+def weight_parts(sz, factor, n1, dgate, n2, dup, dact, hs, g):
     wide = sz.width // NB
     units = dup.shape[1] // NB
     total = wide + 3 * units
     slim = pl.BlockSpec((sz.tokens, wide), lambda i: (0, i))
     broad = pl.BlockSpec((sz.tokens, units), lambda i: (0, i))
-    return pl.pallas_call(
+    return (
         functools.partial(weights_kernel, factor, sz.width // sz.n),
-        grid=(NB,),
-        in_specs=[slim, slim, slim, broad, broad, broad, slim],
-        out_specs=pl.BlockSpec((wide, total), lambda i: (i, 0)),
-        out_shape=jax.ShapeDtypeStruct((sz.width, total), BF16),
-        compiler_params=params(32),
-        cost_estimate=cost(2 * sz.tokens * sz.width * total, 24 * sz.tokens * sz.width),
-        name="weight_grads",
-    )(n1, dgate, n2, dup, dact, hs, g)
+        NB,
+        [slim, slim, slim, broad, broad, broad, slim],
+        [pl.BlockSpec((wide, total), lambda i: (i, 0))],
+        [jax.ShapeDtypeStruct((sz.width, total), BF16)],
+        cost(2 * sz.tokens * sz.width * total, 24 * sz.tokens * sz.width),
+        "weight_grads",
+        n1,
+        dgate,
+        n2,
+        dup,
+        dact,
+        hs,
+        g,
+    )
 
 
 def last_kernel(sz, x_ref, d_ref, first_ref, gain_ref, mix_ref, dgate_ref, dy_ref, out_ref):
@@ -433,26 +555,34 @@
         ).astype(BF16)
 
 
-def last(sz, x, d, first, gain, mix, dgate, dy):
-    tokens = sz.token_spec(sz.width)
-    return pl.pallas_call(
+def last(sz, part, x, d, first, gain, mix, dgate, dy):
+    steps = sz.rows // sz.per
+    skip = part * steps
+    tokens = sz.token_spec(sz.width, skip)
+    return call(
         functools.partial(last_kernel, sz),
-        grid=(sz.rows // sz.per,),
-        in_specs=[
+        steps,
+        [
             tokens,
             sz.sent_spec(),
-            sz.factor_spec(),
+            sz.factor_spec(skip),
             whole((1, sz.width)),
             whole(mix.shape),
             tokens,
             tokens,
         ],
-        out_specs=tokens,
-        out_shape=jax.ShapeDtypeStruct((sz.tokens, sz.width), BF16),
-        compiler_params=params(20),
-        cost_estimate=cost(2 * sz.tokens * sz.width * 384, 10 * sz.tokens * sz.width),
-        name="last",
-    )(x, d, first, gain, mix, dgate, dy)
+        sz.token_spec(sz.width),
+        jax.ShapeDtypeStruct((sz.tokens, sz.width), BF16),
+        cost(2 * sz.tokens * sz.width * 384, 10 * sz.tokens * sz.width),
+        "last",
+        x,
+        d,
+        first,
+        gain,
+        mix,
+        dgate,
+        dy,
+    )
 
 
 def shift(array, by):
@@ -491,29 +621,59 @@
     xa, xb, g = section_input[0], stashed_input[0], output_grad[0]
     factor = 1.0 / math.sqrt(sz.tall * sz.line)
 
-    recv_b = sz.to_columns(front(sz, xb, gain_one, first))
+    everything = (0, rows)
+    weights = (mix, up, act, down)
     wide = expand(sz, factor_second[0], factor_third[0])
-    sent_a = front(sz, xa, gain_one, first)
-    sent_a, recv_b = lax.optimization_barrier((sent_a, recv_b))
-    recv_a = sz.to_columns(sent_a)
-    out_b, mixed_b = middle(sz, recv_b, wide, kernel_here, True)
-    out_b, recv_a = lax.optimization_barrier((out_b, recv_a))
-    rows_b = sz.to_rows(out_b)
-    (out_a,) = middle(sz, recv_a, wide, kernel_here, False)
-    out_a, rows_b = lax.optimization_barrier((out_a, rows_b))
-    rows_a = sz.to_rows(out_a)
-
-    sent, dy, dgate, n1, n2, hs, dup, dact = turn(
-        sz, xb, rows_b, fourth, gain_one, gain_two, mix, up, act, down, g
-    )
-    sent, rows_a = lax.optimization_barrier((sent, rows_a))
-    d_cols = sz.to_columns(sent)
-    next_input = shift(tail(sz, xa, rows_a, fourth, gain_one, gain_two, mix, up, act, down), 1)
-    grads = weight_grads(sz, factor, n1, dgate, n2, dup, dact, hs, g)
-    d_out, spectrum_grad = middle_back(sz, d_cols, wide, kernel_here, mixed_b)
-    d_rows = sz.to_rows(d_out)
-    grads, d_rows = lax.optimization_barrier((grads, d_rows))
-    upstream = shift(last(sz, xb, d_rows, first, gain_one, mix, dgate, dy), -1)
+    (sent_b,) = call(*front_parts(sz, xb, gain_one, first))
+    recv_b, sent_a = call_exchanging(
+        sz, sz.to_send(sent_b), everything, 1, *front_parts(sz, xa, gain_one, first)
+    )
+    recv_a, out_b, mixed_b = call_exchanging(
+        sz,
+        sz.to_send(sent_a),
+        everything,
+        2,
+        *middle_parts(sz, sz.to_flat(recv_b), wide, kernel_here, True),
+    )
+    rows_b, out_a = call_exchanging(
+        sz,
+        sz.from_flat(out_b),
+        everything,
+        3,
+        *middle_parts(sz, sz.to_flat(recv_a), wide, kernel_here, False),
+    )
+    rows_a, sent, dy, dgate, n1, n2, hs, dup, dact = call_exchanging(
+        sz,
+        sz.from_flat(out_a),
+        everything,
+        4,
+        *turn_parts(sz, xb, sz.to_rows(rows_b), fourth, gain_one, gain_two, *weights, g),
+    )
+    d_cols, out = call_exchanging(
+        sz,
+        sz.to_send(sent),
+        everything,
+        5,
+        *tail_parts(sz, xa, sz.to_rows(rows_a), fourth, gain_one, gain_two, *weights),
+    )
+    next_input = shift(out, 1)
+    d_out, spectrum_grad = middle_back(sz, sz.to_flat(d_cols), wide, kernel_here, mixed_b)
+    d_out = sz.from_flat(d_out)
+    halves = 2 if rows % 2 == 0 else 1
+    half = rows // halves
+    sh = Sizes(n, half, cols, width)
+    d_rows, grads = call_exchanging(
+        sz, d_out, (0, half), 6, *weight_parts(sz, factor, n1, dgate, n2, dup, dact, hs, g)
+    )
+    upstream = []
+    for part in range(halves):
+        if part:
+            (d_rows,) = call_exchanging(
+                sz, d_out, (part * half, half), 6 + part, lambda: None, 1, [], [], [], cost(0, 0), "rest"
+            )
+        dx = last(sh, part, xb, sh.to_rows(d_rows), first, gain_one, mix, dgate, dy)
+        upstream.append(shift(dx, -1))
+    upstream = jnp.concatenate(upstream, axis=0)
     grads = lax.psum_scatter(grads, "seq", scatter_dimension=0, tiled=True)
     w, u = width // NB, up.shape[1]
     down_grad = jnp.concatenate(

time: 301 us -> 268 us (0.89)
  Pallas kernels: 73.6 us -> 207 us
  waiting for transfers between devices: 97.2 us -> 28.7 us
  local copies, waits for them, and re-layouts: 54.7 us -> 8.21 us
  blocking collectives: 30.4 us -> 0 us
  starting transfers between devices: 27.9 us -> 6.2 us
    pallas_call x10 -> x12, Pallas kernels: 73.6 us -> 207 us  [the longest x7 182 us: call_exchanging(): pl.pallas_call(kernel, grid=(grid,), in_specs=[pl.BlockSpec(memory_space=...]
    all_to_all x5 -> x0, waiting for transfers between devices: 52.5 us -> none  [the longest x2 27.9 us: to_columns(): lax.all_to_all(array, 'seq', split_axis=0, concat_axis=0, tiled=True)]
    unnamed x86 -> x1, local copies, waits for them, and re-layouts: 50.7 us -> 1.32 us
    all_to_all x1 -> x0, blocking collectives: 30.4 us -> none  [to_columns(): lax.all_to_all(array, 'seq', split_axis=0, concat_axis=0, tiled=True)]
    all_to_all x5 -> x0, starting transfers between devices: 23 us -> none  [the longest x3 13.3 us: to_rows(): lax.all_to_all(array, 'seq', split_axis=0, concat_axis=0, tiled=True)]
    ppermute x2 -> x3, waiting for transfers between devices: 44.7 us -> 28.7 us  [shift(): return lax.ppermute(array, 'section', pairs)]
    another operation x0 -> x3, local copies, waits for them, and re-layouts: none -> 3.66 us  [the longest x2 2.28 us: thin(): grouped = factor.reshape(sz.groups, inner, sz.tall, sz.tall)]
    ppermute x2 -> x3, starting transfers between devices: 4.71 us -> 6.16 us  [shift(): return lax.ppermute(array, 'section', pairs)]
  transfers between devices with their start and end apart: 8 -> 4, of which waited for: 7 -> 2; matrix products, arithmetic and copies ran while one was open for 0% -> 1% of each run, Pallas kernels for 20% -> 9%
where the time goes in v2:
time: 268 us
  Pallas kernels  207 us (77%)
  waiting for transfers between devices  28.7 us (11%)
  between operations  14.1 us (5%)
  local copies, waits for them, and re-layouts  8.21 us (3%)
  starting transfers between devices  6.2 us (2%)
  other arithmetic  3.4 us (1%)
    pallas_call x7, Pallas kernels, call_exchanging(): pl.pallas_call(kernel, grid=(grid,), in_specs=[pl.BlockSpec(memory_space=...  182 us
    ppermute x3, waiting for transfers between devices, shift(): return lax.ppermute(array, 'section', pairs)  28.7 us
    pallas_call x5, Pallas kernels, call(): pl.pallas_call(body, grid=(grid,), in_specs=in_specs, out_specs=out_specs...  25.4 us
    ppermute x3, starting transfers between devices, shift(): return lax.ppermute(array, 'section', pairs)  6.16 us
  transfers between devices with their start and end apart: 4, of which 2 were waited for; matrix products, arithmetic and copies ran while one was open for 1% of the time, Pallas kernels for 9%

profile of v2, /device:TPU:0, one launch (start us, length us, event | category | flops | bytes accessed | tf_op | source)
XLA Modules:
  0.0 267.7 jit_solution(9244906046044615822)
XLA Ops:
  7.2 0.0 reduce-scatter.2.cloned.1.call-start
  7.2 1.1 copy.24
  8.4 1.1 copy.23
  9.5 1.4 copy_bitcast_fusion
  10.9 1.2 pad_maximum_fusion.thin_ref
  12.1 4.7 %expand.1.refs_1_.refs_2_.third_ref.second_ref = bf16[4,2,512,512]{3,2,1,0:T(8,128)(2,1)} custom-call(bf16[4,2,512,64]{3,2,1,0:T(8,128)(2,1)} %pad_maximum_fusion.thin_ref), custom_call_target="tpu_custom_call" | custom-call | flops 268435456 | bytes 4194304 | tf_op jit(solution)/shard_map/expand/pallas_call | solution.py:46
  16.8 4.6 %front.2.send_ref = bf16[8,8,16,1024]{3,2,1,0:T(8,128)(2,1)} custom-call(bf16[1024,1024]{1,0:T(8,128)(2,1)} %bitcast.47, f32[1,1024]{1,0:T(1,128)} %gain_ref.5, bf16[8,128,128]{2,1,0:T(8,128)(2,1)} %bitcast.53), custom_call_target="tpu_custom_call" | custom-call | flops 268435456 | bytes 4194304 | tf_op jit(solution)/shard_map/front/pallas_call | solution.py:46
  21.4 29.2 %front.3 = (bf16[8,8,16,1024]{3,2,1,0:T(8,128)(2,1)}, bf16[8,8,16,1024]{3,2,1,0:T(8,128)(2,1)}) custom-call(bf16[8,8,16,1024]{3,2,1,0:T(8,128)(2,1)} %front.2.send_ref, bf16[1024,1024]{1,0:T(8,128)(2,1)} %bitcast.64, f32[1,1024]{1,0:T(1,128)} %gain_ref.5, bf16[8,128,128]{2,1,0:T(8,128)(2,1)} %bitcast.54), custom_call_target="tpu_custom_call" | custom-call | flops 268435456 | bytes 4194304 | tf_op jit(solution)/shard_map/front/pallas_call | solution.py:112
  50.6 29.4 %middle.2 = (bf16[8,8,16,1024]{3,2,1,0:T(8,128)(2,1)}, bf16[1024,1024]{1,0:T(8,128)(2,1)}, f32[1024,1024]{1,0:T(8,128)}) custom-call(bf16[8,8,16,1024]{3,2,1,0:T(8,128)(2,1)} %get-tuple-element.29.send_ref, bf16[1024,1024]{1,0:T(8,128)(2,1)} %bitcast.59, bf16[4,2,512,512]{3,2,1,0:T(8,128)(2,1)} %expand.1.refs_1_.refs_2_.third_ref.second_ref, ...), custom_call_target="tpu_custom_call" | custom-call | flops 2147483648 | bytes 10485760 | tf_op jit(solution)/shard_map/middle/pallas_call | solution.py:112
  80.0 29.0 %middle.3 = (bf16[8,8,16,1024]{3,2,1,0:T(8,128)(2,1)}, bf16[1024,1024]{1,0:T(8,128)(2,1)}) custom-call(bf16[8,8,16,1024]{3,2,1,0:T(8,128)(2,1)} %bitcast.58, bf16[1024,1024]{1,0:T(8,128)(2,1)} %bitcast.57, bf16[4,2,512,512]{3,2,1,0:T(8,128)(2,1)} %expand.1.refs_1_.refs_2_.third_ref.second_ref, ...), custom_call_target="tpu_custom_call" | custom-call | flops 2147483648 | bytes 10485760 | tf_op jit(solution)/shard_map/middle/pallas_call | solution.py:112
  109.0 31.3 %turn.1 = (bf16[8,8,16,1024]{3,2,1,0:T(8,128)(2,1)}, bf16[8,8,16,1024]{3,2,1,0:T(8,128)(2,1)}, bf16[1024,1024]{1,0:T(8,128)(2,1)}, bf16[1024,1024]{1,0:T(8,128)(...) custom-call(bf16[8,8,16,1024]{3,2,1,0:T(8,128)(2,1)} %bitcast.77, ...), custom_call_target="tpu_custom_call" | custom-call | flops 8589934592 | bytes 31457280 | tf_op jit(solution)/shard_map/turn/pallas_call | solution.py:112
  140.4 29.5 %tail.1 = (bf16[8,8,16,1024]{3,2,1,0:T(8,128)(2,1)}, bf16[1024,1024]{1,0:T(8,128)(2,1)}) custom-call(bf16[8,8,16,1024]{3,2,1,0:T(8,128)(2,1)} %get-tuple-element.35.send_ref, bf16[1024,1024]{1,0:T(8,128)(2,1)} %bitcast.65, bf16[8,8,16,1024]{3,2,1,0:T(8,128)(2,1)} %get-tuple-element.36.refs_1_, bf16[8,128,128]{2,1,0:T(8,128)(2,1)} %bitcast.85, ...), custom_call_target="tpu_custom_call" | custom-call | flops 4294967296 | bytes 8388608 | tf_op jit(solution)/shard_map/tail/pallas_call | solution.py:112
  169.9 7.7 %middle_back.1 = (bf16[1024,1024]{1,0:T(8,128)(2,1)}, bf16[1024,1024]{1,0:T(8,128)(2,1)}) custom-call(bf16[1024,1024]{1,0:T(8,128)(2,1)} %bitcast.69, bf16[4,2,512,512]{3,2,1,0:T(8,128)(2,1)} %expand.1.refs_1_.refs_2_.third_ref.second_ref, bf16[4,2,512,512]{3,2,1,0:T(8,128)(2,1)} %expand.1.refs_1_.refs_2_.third_ref.second_ref, bf16[1024,1024]{1,0:T(8,128)(2,1)} %bitcast.46, ...), custom_call_target="tpu_custom_call" | custom-call | flops 2147483648 | bytes 12582912 | tf_op jit(solution)/shard_map/middle_back/pallas_call | solution.py:46
  177.6 18.5 %weight_grads.1 = (bf16[8,4,16,1024]{3,2,1,0:T(8,128)(2,1)}, bf16[1024,1792]{1,0:T(8,128)(2,1)}) custom-call(bf16[8,8,16,1024]{3,2,1,0:T(8,128)(2,1)} %bitcast.51, bf16[1024,1024]{1,0:T(8,128)(2,1)} %get-tuple-element.41.refs_0_, bf16[1024,1024]{1,0:T(8,128)(2,1)} %get-tuple-element.42.refs_1_.dgate_ref, bf16[1024,1024]{1,0:T(8,128)(2,1)} %get-tuple-element.43.refs_2_, ...), custom_call_target="tpu_custom_call" | custom-call | flops 3758096384 | bytes 25165824 | tf_op jit(solution)/shard_map/weight_grads/pallas_call | solution.py:112
  196.1 0.0 reduce-scatter.2.cloned.1.call-update
  196.1 3.6 %collective-permute-start = (bf16[1024,1024]{1,0:T(8,128)(2,1)}, bf16[1024,1024]{1,0:T(8,128)(2,1)S(1)}, u32[]{:S(2)}, u32[]{:S(2)}) collective-permute-start(bf16[1024,1024]{1,0:T(8,128)(2,1)} %get-tuple-element.37), channel_id=1, source_target_pairs={{0,8},{8,16},{16,24},{1,9},{9,17},{17,25},{2,10},{10,18},{18,26},{... | collective-permute-start | bytes 6291464 | tf_op jit(solution)/shard_map/ppermute | solution.py:591
  199.8 4.2 %last.2 = bf16[512,1024]{1,0:T(8,128)(2,1)} custom-call(bf16[1024,1024]{1,0:T(8,128)(2,1)} %bitcast.49, bf16[8,4,16,1024]{3,2,1,0:T(8,128)(2,1)} %get-tuple-element.47.d_ref, bf16[8,128,128]{2,1,0:T(8,128)(2,1)} %bitcast.55, f32[1,1024]{1,0:T(1,128)} %gain_ref.5, bf16[1024,256]{1,0:T(8,128)(2,1)} %bitcast.62, ...), custom_call_target="tpu_custom_call" | custom-call | flops 402653184 | bytes 5242880 | tf_op jit(solution)/shard_map/last/pallas_call | solution.py:46
  203.9 1.3 collective-permute-start.1
  205.2 14.8 %rest.1.d_ref = bf16[8,4,16,1024]{3,2,1,0:T(8,128)(2,1)} custom-call(bf16[8,8,16,1024]{3,2,1,0:T(8,128)(2,1)} %bitcast.52), custom_call_target="tpu_custom_call" | custom-call | tf_op jit(solution)/shard_map/rest/pallas_call | solution.py:112
  220.0 4.2 %last.3 = bf16[512,1024]{1,0:T(8,128)(2,1)} custom-call(bf16[1024,1024]{1,0:T(8,128)(2,1)} %bitcast.50, bf16[8,4,16,1024]{3,2,1,0:T(8,128)(2,1)} %rest.1.d_ref, bf16[8,128,128]{2,1,0:T(8,128)(2,1)} %bitcast.56, f32[1,1024]{1,0:T(1,128)} %gain_ref.5, bf16[1024,256]{1,0:T(8,128)(2,1)} %bitcast.63, bf16[1024,1024]{1,0:T(8,128)(2,1)} %get-tuple-element.42.refs_1_.dgate_ref, ...), custom_call_target="tpu_custom_call" | custom-call | flops 402653184 | bytes 5242880 | tf_op jit(solution)/shard_map/last/pallas_call | solution.py:46
  224.2 1.3 collective-permute-start.2
  225.5 6.4 %collective-permute-done.1 = bf16[512,1024]{1,0:T(8,128)(2,1)S(1)} collective-permute-done((bf16[512,1024]{1,0:T(8,128)(2,1)}, bf16[512,1024]{1,0:T(8,128)(2,1)S(1)}, u32[]{:S(2)}, u32[]{:S(2)}) %collective-permute-start.1) | collective-permute-done | bytes 1048608 | tf_op jit(solution)/shard_map/ppermute | solution.py:591
  232.0 22.2 %collective-permute-done.2 = bf16[512,1024]{1,0:T(8,128)(2,1)S(1)} collective-permute-done((bf16[512,1024]{1,0:T(8,128)(2,1)}, bf16[512,1024]{1,0:T(8,128)(2,1)S(1)}, u32[]{:S(2)}, u32[]{:S(2)}) %collective-permute-start.2) | collective-permute-done | bytes 1048608 | tf_op jit(solution)/shard_map/ppermute | solution.py:591
  254.2 1.5 maximum_bitcast_fusion
  255.7 0.0 collective-permute-done
  255.7 0.0 reduce-scatter.2.cloned.1.call-done
  255.7 1.5 fusion
  257.2 0.7 maximum_bitcast_fusion.1
  257.9 1.7 slice_bitcast_fusion
  259.6 1.3 copy.28
Async XLA Ops:
  7.2 248.5 %reduce-scatter.2.cloned.1.call-start = ((), (), s32[]{:S(2)}) async-start(), calls=%async_computation.1 | async-start | bytes 4128768 | tf_op jit(solution)/shard_map/reduce_scatter | solution.py:677
  196.1 59.5 %collective-permute-start = (bf16[1024,1024]{1,0:T(8,128)(2,1)}, bf16[1024,1024]{1,0:T(8,128)(2,1)S(1)}, u32[]{:S(2)}, u32[]{:S(2)}) collective-permute-start(bf16[1024,1024]{1,0:T(8,128)(2,1)} %get-tuple-element.37), channel_id=1, source_target_pairs={{0,8},{8,16},{16,24},{1,9},{9,17},{17,25},{2,10},{10,18},{18,26},{... | collective-permute-start | bytes 6291464 | tf_op jit(solution)/shard_map/ppermute | solution.py:591
  203.9 28.0 %collective-permute-start.1 = (bf16[512,1024]{1,0:T(8,128)(2,1)}, bf16[512,1024]{1,0:T(8,128)(2,1)S(1)}, u32[]{:S(2)}, u32[]{:S(2)}) collective-permute-start(bf16[512,1024]{1,0:T(8,128)(2,1)} %last.2), channel_id=1, source_target_pairs={{8,0},{16,8},{24,16},{9,1},{17,9},{25,17},{10,2},{18,10},{26,18},{... | collective-permute-start | bytes 3145736 | tf_op jit(solution)/shard_map/ppermute | solution.py:591
  224.2 29.9 %collective-permute-start.2 = (bf16[512,1024]{1,0:T(8,128)(2,1)}, bf16[512,1024]{1,0:T(8,128)(2,1)S(1)}, u32[]{:S(2)}, u32[]{:S(2)}) collective-permute-start(bf16[512,1024]{1,0:T(8,128)(2,1)} %last.3), channel_id=1, source_target_pairs={{8,0},{16,8},{24,16},{9,1},{17,9},{25,17},{10,2},{18,10},{26,18},{... | collective-permute-start | bytes 3145736 | tf_op jit(solution)/shard_map/ppermute | solution.py:591
Sparse Core Ops, SparseCore 0:
  196.3 50.9 reduce-scatter.1

commit v3 on v2

--- a/solution.py
+++ b/solution.py
@@ -57,6 +57,68 @@
     )(*args)
 
 
+def exchange(n, source, target, send_sem, recv_sem, own_sem):
+    me = lax.axis_index("seq")
+    chips = n // 2 if n % 2 == 0 else n
+    cores = n // chips
+    chip, core = me // cores, lax.rem(me, cores)
+
+    def other(r):
+        if chips == 4:
+            return (chip, chip + 1 - 2 * lax.rem(chip, 2), lax.rem(chip + 2, 4), 3 - chip)[r]
+        return lax.rem(chip + r, chips)
+
+    def copy_to(far_chip, relation, c):
+        peer = far_chip * cores + lax.rem(core + c, cores)
+        index = relation * cores + c - 1
+        return pltpu.make_async_remote_copy(
+            src_ref=source(peer),
+            dst_ref=target,
+            send_sem=send_sem(index),
+            recv_sem=recv_sem(index),
+            device_id={"seq": peer},
+            device_id_type=pl.DeviceIdType.MESH,
+        )
+
+    def own_copy():
+        return pltpu.make_async_copy(
+            source(me), target, own_sem
+        )
+
+    def start_all():
+        relations = [(other(r), r) for r in range(1, chips)]
+        if chips == 4 and cores == 2:
+            one, two = relations[0][0], relations[1][0]
+            relations[0] = (one + core * (two - one), 1 + core)
+            relations[1] = (two + core * (one - two), 2 - core)
+        for far_chip, r in relations:
+            for c in range(cores):
+                copy_to(far_chip, r, c).start()
+        for c in range(1, cores):
+            copy_to(chip, 0, c).start()
+        own_copy().start()
+
+    def wait_all():
+        own_copy().wait()
+        for r in range(chips):
+            for c in range(cores):
+                if r or c:
+                    copy_to(other(r), r, c).wait()
+
+    return start_all, wait_all
+
+
+def greet(n, others=()):
+    barrier = pltpu.get_barrier_semaphore()
+    me = lax.axis_index("seq")
+    devices = [{"seq": lax.rem(me + k, n)} for k in range(1, n)] + list(others)
+    for device in devices:
+        pl.semaphore_signal(
+            barrier, inc=1, device_id=device, device_id_type=pl.DeviceIdType.MESH
+        )
+    pl.semaphore_wait(barrier, len(devices))
+
+
 def call_exchanging(
     sz, send, span, cid, body, grid, in_specs, out_specs, out_shape, price, name, *args
 ):
@@ -70,43 +132,25 @@
         step = pl.program_id(0)
         me = lax.axis_index("seq")
 
-        def copies():
-            own = pltpu.make_async_copy(
-                send_ref.at[me, pl.ds(span[0], span[1])], recv_ref.at[me], own_sem
-            )
-            far = [
-                pltpu.make_async_remote_copy(
-                    src_ref=send_ref.at[lax.rem(me + k, n), pl.ds(span[0], span[1])],
-                    dst_ref=recv_ref.at[me],
-                    send_sem=send_sem.at[k - 1],
-                    recv_sem=recv_sem.at[k - 1],
-                    device_id={"seq": lax.rem(me + k, n)},
-                    device_id_type=pl.DeviceIdType.MESH,
-                )
-                for k in range(1, n)
-            ]
-            return far + [own]
+        start_all, wait_all = exchange(
+            n,
+            lambda peer: send_ref.at[peer, pl.ds(span[0], span[1])],
+            recv_ref.at[me],
+            lambda k: send_sem.at[k],
+            lambda k: recv_sem.at[k],
+            own_sem,
+        )
 
         @pl.when(step == 0)
         def _():
-            barrier = pltpu.get_barrier_semaphore()
-            for k in range(1, n):
-                pl.semaphore_signal(
-                    barrier,
-                    inc=1,
-                    device_id={"seq": lax.rem(me + k, n)},
-                    device_id_type=pl.DeviceIdType.MESH,
-                )
-            pl.semaphore_wait(barrier, n - 1)
-            for copy in copies():
-                copy.start()
+            greet(n)
+            start_all()
 
         body(*ins, *outs)
 
         @pl.when(step == grid - 1)
         def _():
-            for copy in copies():
-                copy.wait()
+            wait_all()
 
     shape = (n, span[1]) + send.shape[2:]
     return pl.pallas_call(
@@ -220,38 +264,50 @@
     )
 
 
-def expand_kernel(cols, tall, thin_ref, wide_ref):
+def expand_piece(factor, cols, tall):
     size = tall * cols
+
+    def index(axis):
+        return lax.broadcasted_iota(jnp.int32, (size, size), axis)
+
+    swap = (index(0) // cols == index(1) % tall) & (index(0) % cols == index(1) // tall)
+    swap = swap.astype(F32).astype(BF16)
+    thin = dot(swap, factor.reshape(size, tall)).astype(BF16)
     pick = lax.broadcasted_iota(jnp.int32, (tall, size), 1) // cols
     pick = (pick == lax.broadcasted_iota(jnp.int32, (tall, size), 0)).astype(F32).astype(BF16)
-    left = lax.broadcasted_iota(jnp.int32, (size, size), 0) % cols
-    right = lax.broadcasted_iota(jnp.int32, (size, size), 1) % cols
-    for g in range(thin_ref.shape[1]):
-        spread = dot(thin_ref[0, g], pick)
-        wide_ref[0, g] = jnp.where(left == right, spread, 0.0).astype(BF16)
-
-
-def expand(sz, second, third):
+    return jnp.where(index(0) % cols == index(1) % cols, dot(thin, pick), 0.0)
+
+
+def front_expand_kernel(sz, steps, x_ref, gain_ref, first_ref, second, third, sent_ref, wide_ref):
+    front_kernel(sz, x_ref, gain_ref, first_ref, sent_ref)
     inner = sz.cols // sz.groups
-    size = sz.tall * inner
-
-    def thin(factor, order):
-        grouped = factor.reshape(sz.groups, inner, sz.tall, sz.tall)
-        return grouped.transpose(order).reshape(sz.groups, size, sz.tall)
-
-    ahead, back = (0, 2, 1, 3), (0, 3, 1, 2)
-    stack = jnp.stack(
-        [thin(second, ahead), thin(third, ahead), thin(third, back), thin(second, back)]
-    )
-    return call(
-        functools.partial(expand_kernel, inner, sz.tall),
-        4,
-        [pl.BlockSpec((1, sz.groups, size, sz.tall), lambda i: (i, 0, 0, 0))],
-        pl.BlockSpec((1, sz.groups, size, size), lambda i: (i, 0, 0, 0)),
-        jax.ShapeDtypeStruct((4, sz.groups, size, size), BF16),
-        cost(8 * sz.groups * size * size * sz.tall, 8 * sz.groups * size * size),
-        "expand",
-        stack,
+    step = pl.program_id(0)
+    for k in range(2 * sz.groups):
+
+        @pl.when(step == k % steps)
+        def _():
+            which, g = k // sz.groups, k % sz.groups
+            factor = (second, third)[which][g * inner : (g + 1) * inner]
+            piece = expand_piece(factor, inner, sz.tall)
+            wide_ref[which, g] = piece.astype(BF16)
+            wide_ref[3 - which, g] = piece.T.astype(BF16)
+
+
+def front_expand_parts(sz, x, gain, first, second, third):
+    body, grid, ins, outs, shapes, price, name, *args = front_parts(sz, x, gain, first)
+    size = sz.tall * sz.cols // sz.groups
+    wide = (4, sz.groups, size, size)
+    return (
+        functools.partial(front_expand_kernel, sz, grid),
+        grid,
+        ins + [whole(second.shape), whole(third.shape)],
+        outs + [whole(wide)],
+        shapes + [jax.ShapeDtypeStruct(wide, BF16)],
+        price,
+        name,
+        *args,
+        second,
+        third,
     )
 
 
@@ -585,6 +641,207 @@
     )
 
 
+def join(one, two):
+    a, b = len(one[2]), len(two[2])
+    c = len(one[3])
+
+    def body(*refs):
+        ins, outs = refs[: a + b], refs[a + b :]
+        one[0](*ins[:a], *outs[:c])
+        two[0](*ins[a:], *outs[c:])
+
+    return (
+        (body, one[1], one[2] + two[2], one[3] + two[3], one[4] + two[4], one[5], one[6])
+        + tuple(one[7:])
+        + tuple(two[7:])
+    )
+
+
+def finish_kernel(
+    sz,
+    parts,
+    send_ref,
+    x_ref,
+    first_ref,
+    gain_ref,
+    mix_ref,
+    dgate_ref,
+    dy_ref,
+    out_ref,
+    recv,
+    dx,
+    zero,
+    send_sem,
+    recv_sem,
+    own_sem,
+    up_send,
+    up_recv,
+    zero_sem,
+):
+    step = pl.program_id(0)
+    me, section = lax.axis_index("seq"), lax.axis_index("section")
+    sections = lax.axis_size("section")
+    some = sz.rows // parts
+    wide = sz.width // NB
+
+    def part_exchange(p):
+        return exchange(
+            sz.n,
+            lambda peer: send_ref.at[peer, pl.ds(p * some, some)],
+            recv.at[p, me],
+            lambda k: send_sem.at[p, k],
+            lambda k: recv_sem.at[p, k],
+            own_sem.at[p],
+        )
+
+    def up_copy(p):
+        return pltpu.make_async_remote_copy(
+            src_ref=dx.at[p],
+            dst_ref=out_ref.at[p],
+            send_sem=up_send.at[p],
+            recv_sem=up_recv.at[p],
+            device_id={"section": lax.rem(section + sections - 1, sections)},
+            device_id_type=pl.DeviceIdType.MESH,
+        )
+
+    def zero_copy(p):
+        return pltpu.make_async_copy(zero, out_ref.at[p], zero_sem.at[p])
+
+    top = section == sections - 1
+
+    @pl.when(step == 0)
+    def _():
+        greet(
+            sz.n,
+            [
+                {"section": lax.rem(section + 1, sections)},
+                {"section": lax.rem(section + sections - 1, sections)},
+            ],
+        )
+        for p in range(parts):
+            part_exchange(p)[0]()
+
+        @pl.when(top)
+        def _():
+            zero[...] = jnp.zeros_like(zero)
+            for p in range(parts):
+                zero_copy(p).start()
+
+    gain = gain_ref[...]
+    gated, scales = [], []
+    for r in range(some):
+        at = pl.ds(r * sz.line, sz.line)
+        gated.append(
+            jnp.concatenate(
+                [
+                    dot_t(
+                        dgate_ref[at, b * wide : (b + 1) * wide],
+                        mix_ref[b * wide : (b + 1) * wide, :],
+                    )
+                    for b in range(NB)
+                ],
+                axis=1,
+            )
+        )
+        scales.append(rms_scale(x_ref[at, :].astype(F32)))
+    part_exchange(step)[1]()
+    for r in range(some):
+        at = pl.ds(r * sz.line, sz.line)
+        d = recv[step, :, r].reshape(sz.line, sz.width)
+        d_normed = t_dot(first_ref[r], d) + gated[r]
+        x = x_ref[at, :].astype(F32)
+        dx[step, at, :] = (
+            dy_ref[at, :].astype(F32) + norm_back(x, scales[r], gain, d_normed)
+        ).astype(BF16)
+
+    @pl.when(section > 0)
+    def _():
+        up_copy(step).start()
+
+    @pl.when(step == parts - 1)
+    def _():
+        @pl.when(section > 0)
+        def _():
+            for p in range(parts):
+                up_copy(p).wait_send()
+
+        @pl.when(section < sections - 1)
+        def _():
+            for p in range(parts):
+                up_copy(p).wait_recv()
+
+        @pl.when(top)
+        def _():
+            for p in range(parts):
+                zero_copy(p).wait()
+
+
+def finish(sz, parts, cid, d, x, first, gain, mix, dgate, dy):
+    some = sz.rows // parts
+    tokens = some * sz.line
+    strip = pl.BlockSpec((tokens, sz.width), lambda i: (i, 0))
+    out = pl.pallas_call(
+        functools.partial(finish_kernel, sz, parts),
+        grid=(parts,),
+        in_specs=[
+            pl.BlockSpec(memory_space=pl.ANY),
+            strip,
+            pl.BlockSpec((some, sz.line, sz.line), lambda i: (i, 0, 0)),
+            whole((1, sz.width)),
+            whole(mix.shape),
+            strip,
+            strip,
+        ],
+        out_specs=pl.BlockSpec(memory_space=pl.ANY),
+        out_shape=jax.ShapeDtypeStruct((parts, tokens, sz.width), BF16),
+        scratch_shapes=[
+            pltpu.VMEM((parts, sz.n, some, sz.cols, sz.width), BF16),
+            pltpu.VMEM((parts, tokens, sz.width), BF16),
+            pltpu.VMEM((tokens, sz.width), BF16),
+            pltpu.SemaphoreType.DMA((parts, sz.n - 1)),
+            pltpu.SemaphoreType.DMA((parts, sz.n - 1)),
+            pltpu.SemaphoreType.DMA((parts,)),
+            pltpu.SemaphoreType.DMA((parts,)),
+            pltpu.SemaphoreType.DMA((parts,)),
+            pltpu.SemaphoreType.DMA((parts,)),
+        ],
+        compiler_params=pltpu.CompilerParams(
+            dimension_semantics=("arbitrary",),
+            vmem_limit_bytes=VMEM,
+            collective_id=cid,
+            has_side_effects=True,
+        ),
+        cost_estimate=cost(2 * sz.tokens * sz.width * 384, 10 * sz.tokens * sz.width),
+        name="finish",
+    )(d, x, first, gain, mix, dgate, dy)
+    return out.reshape(sz.tokens, sz.width)
+
+
+def split_kernel(wide, units, total, mix_ref, up_ref, act_ref, down_ref):
+    mix_ref[...] = total[:, :wide]
+    up_ref[...] = total[:, wide : wide + units]
+    act_ref[...] = total[:, wide + units : wide + 2 * units]
+    share = total.shape[0]
+    for k in range(units // wide):
+        at = wide + 2 * units + k * wide
+        down_ref[k * share : (k + 1) * share, :] = total[:, at : at + wide]
+
+
+def split_grads(total, wide, units):
+    share = total.shape[0]
+    shapes = [(share, wide), (share, units), (share, units), (share * units // wide, wide)]
+    return call(
+        functools.partial(split_kernel, wide, units),
+        1,
+        [whole(total.shape)],
+        [whole(shape) for shape in shapes],
+        [jax.ShapeDtypeStruct(shape, BF16) for shape in shapes],
+        cost(0, 4 * share * (wide + 3 * units)),
+        "split_grads",
+        total,
+    )
+
+
 def shift(array, by):
     length = lax.axis_size("section")
     pairs = [(i, i + by) for i in range(length) if 0 <= i + by < length]
@@ -623,10 +880,13 @@
 
     everything = (0, rows)
     weights = (mix, up, act, down)
-    wide = expand(sz, factor_second[0], factor_third[0])
     (sent_b,) = call(*front_parts(sz, xb, gain_one, first))
-    recv_b, sent_a = call_exchanging(
-        sz, sz.to_send(sent_b), everything, 1, *front_parts(sz, xa, gain_one, first)
+    recv_b, sent_a, wide = call_exchanging(
+        sz,
+        sz.to_send(sent_b),
+        everything,
+        1,
+        *front_expand_parts(sz, xa, gain_one, first, factor_second[0], factor_third[0]),
     )
     recv_a, out_b, mixed_b = call_exchanging(
         sz,
@@ -649,45 +909,38 @@
         4,
         *turn_parts(sz, xb, sz.to_rows(rows_b), fourth, gain_one, gain_two, *weights, g),
     )
-    d_cols, out = call_exchanging(
-        sz,
-        sz.to_send(sent),
-        everything,
-        5,
-        *tail_parts(sz, xa, sz.to_rows(rows_a), fourth, gain_one, gain_two, *weights),
-    )
+    work = tail_parts(sz, xa, sz.to_rows(rows_a), fourth, gain_one, gain_two, *weights)
+    more = weight_parts(sz, factor, n1, dgate, n2, dup, dact, hs, g)
+    if work[1] == more[1]:
+        d_cols, out, grads = call_exchanging(
+            sz, sz.to_send(sent), everything, 5, *join(work, more)
+        )
+    else:
+        d_cols, out = call_exchanging(sz, sz.to_send(sent), everything, 5, *work)
+        (grads,) = call(*more)
     next_input = shift(out, 1)
     d_out, spectrum_grad = middle_back(sz, sz.to_flat(d_cols), wide, kernel_here, mixed_b)
     d_out = sz.from_flat(d_out)
-    halves = 2 if rows % 2 == 0 else 1
-    half = rows // halves
-    sh = Sizes(n, half, cols, width)
-    d_rows, grads = call_exchanging(
-        sz, d_out, (0, half), 6, *weight_parts(sz, factor, n1, dgate, n2, dup, dact, hs, g)
-    )
-    upstream = []
-    for part in range(halves):
-        if part:
-            (d_rows,) = call_exchanging(
-                sz, d_out, (part * half, half), 6 + part, lambda: None, 1, [], [], [], cost(0, 0), "rest"
-            )
-        dx = last(sh, part, xb, sh.to_rows(d_rows), first, gain_one, mix, dgate, dy)
-        upstream.append(shift(dx, -1))
-    upstream = jnp.concatenate(upstream, axis=0)
-    grads = lax.psum_scatter(grads, "seq", scatter_dimension=0, tiled=True)
-    w, u = width // NB, up.shape[1]
-    down_grad = jnp.concatenate(
-        [grads[:, w + 2 * u + k * w : w + 2 * u + (k + 1) * w] for k in range(u // w)], axis=0
-    )
+    parts = max(k for k in (1, 2, 4) if rows % k == 0)
+    some = rows // parts
+    sp = Sizes(n, some, cols, width)
+    grads, d_out = lax.optimization_barrier((grads, d_out))
+    total = lax.psum_scatter(grads, "seq", scatter_dimension=0, tiled=True)
+    if sz.aligned:
+        upstream = finish(sz, parts, 6, d_out, xb, first, gain_one, mix, dgate, dy)
+    else:
+        dx = []
+        for part in range(parts):
+            work = (lambda: None, 1, [], [], [], cost(0, 0), "rest")
+            (d_rows,) = call_exchanging(sz, d_out, (part * some, some), 6 + part, *work)
+            dx.append(last(sp, part, xb, sp.to_rows(d_rows), first, gain_one, mix, dgate, dy))
+        upstream = shift(jnp.concatenate(dx, axis=0), -1)
+    grads = split_grads(total, width // NB, up.shape[1])
     return (
         next_input[None],
         upstream[None],
         spectrum_grad.reshape(spectrum.shape),
-        grads[None, :, :w],
-        grads[None, :, w : w + u],
-        grads[None, :, w + u : w + 2 * u],
-        down_grad[None],
-    )
+    ) + tuple(grad[None] for grad in grads)
 
 
 def solution(mesh):

time: 268 us -> 249 us (0.929)
  waiting for transfers between devices: 28.7 us -> 0.04 us
  Pallas kernels: 207 us -> 227 us
  local copies, waits for them, and re-layouts: 8.21 us -> 3.67 us
  other arithmetic: 3.4 us -> 0 us
    pallas_call x0 -> x1, Pallas kernels: none -> 60.3 us  [finish(): pl.pallas_call(functools.partial(finish_kernel, sz, parts), grid=(parts,)...]
    pallas_call x7 -> x5, Pallas kernels: 182 us -> 153 us  [call_exchanging(): pl.pallas_call(kernel, grid=(grid,), in_specs=[pl.BlockSpec(memory_space=...]
    ppermute x3 -> x1, waiting for transfers between devices: 28.7 us -> 0.01 us  [shift(): return lax.ppermute(array, 'section', pairs)]
    pallas_call x5 -> x3, Pallas kernels: 25.4 us -> 14.1 us  [call(): pl.pallas_call(body, grid=(grid,), in_specs=in_specs, out_specs=out_specs...]
    another operation x3 -> x0, local copies, waits for them, and re-layouts: 3.66 us -> none  [the longest x2 2.28 us: thin(): grouped = factor.reshape(sz.groups, inner, sz.tall, sz.tall)]
    ppermute x3 -> x1, starting transfers between devices: 6.16 us -> 3.61 us  [shift(): return lax.ppermute(array, 'section', pairs)]
  transfers between devices with their start and end apart: 4 -> 2, of which waited for: 2 -> 0; matrix products, arithmetic and copies ran while one was open for 1% -> 0% of each run, Pallas kernels for 9% -> 24%
where the time goes in v3:
time: 249 us
  Pallas kernels  227 us (91%)
  between operations  14.1 us (6%)
  local copies, waits for them, and re-layouts  3.67 us (1%)
  starting transfers between devices  3.65 us (1%)
    pallas_call x5, Pallas kernels, call_exchanging(): pl.pallas_call(kernel, grid=(grid,), in_specs=[pl.BlockSpec(memory_space=...  153 us
    pallas_call x1, Pallas kernels, finish(): pl.pallas_call(functools.partial(finish_kernel, sz, parts), grid=(parts,)...  60.3 us
    pallas_call x3, Pallas kernels, call(): pl.pallas_call(body, grid=(grid,), in_specs=in_specs, out_specs=out_specs...  14.1 us
  transfers between devices with their start and end apart: 2, of which 0 were waited for; matrix products, arithmetic and copies ran while one was open for 0% of the time, Pallas kernels for 24%

profile of v3, /device:TPU:0, one launch (start us, length us, event | category | flops | bytes accessed | tf_op | source)
XLA Modules:
  0.0 248.6 jit_solution(6313982507608247307)
XLA Ops:
  7.2 0.0 reduce-scatter.2.cloned.1.call-start
  7.2 4.6 %front.2.send_ref = bf16[8,8,16,1024]{3,2,1,0:T(8,128)(2,1)} custom-call(bf16[1024,1024]{1,0:T(8,128)(2,1)} %bitcast.28, f32[1,1024]{1,0:T(1,128)} %gain_ref.3, bf16[8,128,128]{2,1,0:T(8,128)(2,1)} %bitcast.34), custom_call_target="tpu_custom_call" | custom-call | flops 268435456 | bytes 4194304 | tf_op jit(solution)/shard_map/front/pallas_call | solution.py:46
  11.8 31.2 %front.3 = (bf16[8,8,16,1024]{3,2,1,0:T(8,128)(2,1)}, bf16[8,8,16,1024]{3,2,1,0:T(8,128)(2,1)}, bf16[4,2,512,512]{3,2,1,0:T(8,128)(2,1)}) custom-call(bf16[8,8,16,1024]{3,2,1,0:T(8,128)(2,1)} %front.2.send_ref, bf16[1024,1024]{1,0:T(8,128)(2,1)} %bitcast.31, f32[1,1024]{1,0:T(1,128)} %gain_ref.3, bf16[8,128,128]{2,1,0:T(8,128)(2,1)} %bitcast.35, ...), custom_call_target="tpu_custom_call" | custom-call | flops 268435456 | bytes 4194304 | tf_op jit(solution)/shard_map/front/pallas_call | solution.py:156
  43.0 29.5 %middle.2 = (bf16[8,8,16,1024]{3,2,1,0:T(8,128)(2,1)}, bf16[1024,1024]{1,0:T(8,128)(2,1)}, f32[1024,1024]{1,0:T(8,128)}) custom-call(bf16[8,8,16,1024]{3,2,1,0:T(8,128)(2,1)} %get-tuple-element.35.send_ref, bf16[1024,1024]{1,0:T(8,128)(2,1)} %bitcast.43, bf16[4,2,512,512]{3,2,1,0:T(8,128)(2,1)} %get-tuple-element.37.refs_1_.refs_2_.third_ref.second_ref, ...), custom_call_target="tpu_custom_call" | custom-call | flops 2147483648 | bytes 10485760 | tf_op jit(solution)/shard_map/middle/pallas_call | solution.py:156
  72.5 29.1 %middle.3 = (bf16[8,8,16,1024]{3,2,1,0:T(8,128)(2,1)}, bf16[1024,1024]{1,0:T(8,128)(2,1)}) custom-call(bf16[8,8,16,1024]{3,2,1,0:T(8,128)(2,1)} %bitcast.45, bf16[1024,1024]{1,0:T(8,128)(2,1)} %bitcast.44, bf16[4,2,512,512]{3,2,1,0:T(8,128)(2,1)} %get-tuple-element.37.refs_1_.refs_2_.third_ref.second_ref, ...), custom_call_target="tpu_custom_call" | custom-call | flops 2147483648 | bytes 10485760 | tf_op jit(solution)/shard_map/middle/pallas_call | solution.py:156
  101.6 31.4 %turn.1 = (bf16[8,8,16,1024]{3,2,1,0:T(8,128)(2,1)}, bf16[8,8,16,1024]{3,2,1,0:T(8,128)(2,1)}, bf16[1024,1024]{1,0:T(8,128)(2,1)}, bf16[1024,1024]{1,0:T(8,128)(...) custom-call(bf16[8,8,16,1024]{3,2,1,0:T(8,128)(2,1)} %bitcast.59, ...), custom_call_target="tpu_custom_call" | custom-call | flops 8589934592 | bytes 31457280 | tf_op jit(solution)/shard_map/turn/pallas_call | solution.py:156
  133.1 31.5 %tail.1 = (bf16[8,8,16,1024]{3,2,1,0:T(8,128)(2,1)}, bf16[1024,1024]{1,0:T(8,128)(2,1)}, bf16[1024,1792]{1,0:T(8,128)(2,1)}) custom-call(bf16[8,8,16,1024]{3,2,1,0:T(8,128)(2,1)} %get-tuple-element.42.send_ref, bf16[1024,1024]{1,0:T(8,128)(2,1)} %bitcast.32, bf16[8,8,16,1024]{3,2,1,0:T(8,128)(2,1)} %get-tuple-element.43.refs_1_, ...), custom_call_target="tpu_custom_call" | custom-call | flops 4294967296 | bytes 8388608 | tf_op jit(solution)/shard_map/tail/pallas_call | solution.py:156
  164.6 7.7 %middle_back.1 = (bf16[1024,1024]{1,0:T(8,128)(2,1)}, bf16[1024,1024]{1,0:T(8,128)(2,1)}) custom-call(bf16[1024,1024]{1,0:T(8,128)(2,1)} %bitcast.47, bf16[4,2,512,512]{3,2,1,0:T(8,128)(2,1)} %get-tuple-element.37.refs_1_.refs_2_.third_ref.second_ref, bf16[4,2,512,512]{3,2,1,0:T(8,128)(2,1)} %get-tuple-element.37.refs_1_.refs_2_.third_ref.second_ref, ...), custom_call_target="tpu_custom_call" | custom-call | flops 2147483648 | bytes 12582912 | tf_op jit(solution)/shard_map/middle_back/pallas_call | solution.py:46
  172.3 0.0 reduce-scatter.2.cloned.1.call-update
  172.4 3.6 %collective-permute-start = (bf16[1024,1024]{1,0:T(8,128)(2,1)}, bf16[1024,1024]{1,0:T(8,128)(2,1)S(1)}, u32[]{:S(2)}, u32[]{:S(2)}) collective-permute-start(bf16[1024,1024]{1,0:T(8,128)(2,1)} %get-tuple-element.50), channel_id=1, source_target_pairs={{0,8},{8,16},{16,24},{1,9},{9,17},{17,25},{2,10},{10,18},{18,26},{... | collective-permute-start | bytes 6291464 | tf_op jit(solution)/shard_map/ppermute | solution.py:848
  176.0 60.3 %finish.1 = bf16[4,256,1024]{2,1,0:T(8,128)(2,1)} custom-call(bf16[8,8,16,1024]{3,2,1,0:T(8,128)(2,1)} %bitcast.42, bf16[1024,1024]{1,0:T(8,128)(2,1)} %bitcast.30, bf16[8,128,128]{2,1,0:T(8,128)(2,1)} %bitcast.36, f32[1,1024]{1,0:T(1,128)} %gain_ref.3, bf16[1024,256]{1,0:T(8,128)(2,1)} %bitcast.39, bf16[1024,1024]{1,0:T(8,128)(2,1)} %get-tuple-element.45.refs_10_.dgate_ref, ...), custom_call_target="tpu_custom_call" | custom-call | flops 805306368 | bytes 10485760 | tf_op jit(solution)/shard_map/finish/pallas_call | solution.py:783
  236.3 0.0 collective-permute-done
  236.3 0.0 reduce-scatter.2.cloned.1.call-done.total
  236.3 1.8 split_grads.1
  238.1 0.0 copy-start
  238.1 1.3 copy.23
  239.4 1.0 copy-done
  240.5 1.3 copy.24
Async XLA Ops:
  7.2 229.2 %reduce-scatter.2.cloned.1.call-start = ((), (), s32[]{:S(2)}) async-start(), calls=%async_computation.1 | async-start | bytes 4128768 | tf_op jit(solution)/shard_map/reduce_scatter | solution.py:928
  172.4 63.9 %collective-permute-start = (bf16[1024,1024]{1,0:T(8,128)(2,1)}, bf16[1024,1024]{1,0:T(8,128)(2,1)S(1)}, u32[]{:S(2)}, u32[]{:S(2)}) collective-permute-start(bf16[1024,1024]{1,0:T(8,128)(2,1)} %get-tuple-element.50), channel_id=1, source_target_pairs={{0,8},{8,16},{16,24},{1,9},{9,17},{17,25},{2,10},{10,18},{18,26},{... | collective-permute-start | bytes 6291464 | tf_op jit(solution)/shard_map/ppermute | solution.py:848
  238.1 2.3 copy-start
Sparse Core Ops, SparseCore 0:
  172.5 55.5 reduce-scatter.1

commit v4 on v3

--- a/solution.py
+++ b/solution.py
@@ -718,8 +718,7 @@
                 {"section": lax.rem(section + sections - 1, sections)},
             ],
         )
-        for p in range(parts):
-            part_exchange(p)[0]()
+        part_exchange(0)[0]()
 
         @pl.when(top)
         def _():
@@ -745,6 +744,16 @@
         )
         scales.append(rms_scale(x_ref[at, :].astype(F32)))
     part_exchange(step)[1]()
+
+    @pl.when(step == 0)
+    def _():
+        for p in range(1, min(parts, 3)):
+            part_exchange(p)[0]()
+
+    @pl.when((step > 0) & (step + 2 < parts))
+    def _():
+        part_exchange(step + 2)[0]()
+
     for r in range(some):
         at = pl.ds(r * sz.line, sz.line)
         d = recv[step, :, r].reshape(sz.line, sz.width)
@@ -921,7 +930,7 @@
     next_input = shift(out, 1)
     d_out, spectrum_grad = middle_back(sz, sz.to_flat(d_cols), wide, kernel_here, mixed_b)
     d_out = sz.from_flat(d_out)
-    parts = max(k for k in (1, 2, 4) if rows % k == 0)
+    parts = max(k for k in (1, 2, 4, 8) if rows % k == 0)
     some = rows // parts
     sp = Sizes(n, some, cols, width)
     grads, d_out = lax.optimization_barrier((grads, d_out))

time: 249 us -> 247 us (level)
  no operation moved by 1% of the time
where the time goes in v4:
time: 247 us; the launch traced here: 246 us
  Pallas kernels  225 us (91%)
  between operations  14.1 us (6%)
  local copies, waits for them, and re-layouts  3.67 us (1%)
  starting transfers between devices  3.65 us (1%)
    pallas_call x5, Pallas kernels, call_exchanging(): pl.pallas_call(kernel, grid=(grid,), in_specs=[pl.BlockSpec(memory_space=...  153 us
    pallas_call x1, Pallas kernels, finish(): pl.pallas_call(functools.partial(finish_kernel, sz, parts), grid=(parts,)...  58 us
    pallas_call x3, Pallas kernels, call(): pl.pallas_call(body, grid=(grid,), in_specs=in_specs, out_specs=out_specs...  14.1 us
  transfers between devices with their start and end apart: 2, of which 0 were waited for; matrix products, arithmetic and copies ran while one was open for 0% of the time, Pallas kernels for 24%

profile of v4, /device:TPU:0, one launch (start us, length us, event | category | flops | bytes accessed | tf_op | source)
XLA Modules:
  0.0 246.4 jit_solution(2995433519965001559)
XLA Ops:
  7.2 0.0 reduce-scatter.2.cloned.1.call-start
  7.2 4.6 %front.2.send_ref = bf16[8,8,16,1024]{3,2,1,0:T(8,128)(2,1)} custom-call(bf16[1024,1024]{1,0:T(8,128)(2,1)} %bitcast.28, f32[1,1024]{1,0:T(1,128)} %gain_ref.3, bf16[8,128,128]{2,1,0:T(8,128)(2,1)} %bitcast.34), custom_call_target="tpu_custom_call" | custom-call | flops 268435456 | bytes 4194304 | tf_op jit(solution)/shard_map/front/pallas_call | solution.py:46
  11.8 31.2 %front.3 = (bf16[8,8,16,1024]{3,2,1,0:T(8,128)(2,1)}, bf16[8,8,16,1024]{3,2,1,0:T(8,128)(2,1)}, bf16[4,2,512,512]{3,2,1,0:T(8,128)(2,1)}) custom-call(bf16[8,8,16,1024]{3,2,1,0:T(8,128)(2,1)} %front.2.send_ref, bf16[1024,1024]{1,0:T(8,128)(2,1)} %bitcast.31, f32[1,1024]{1,0:T(1,128)} %gain_ref.3, bf16[8,128,128]{2,1,0:T(8,128)(2,1)} %bitcast.35, ...), custom_call_target="tpu_custom_call" | custom-call | flops 268435456 | bytes 4194304 | tf_op jit(solution)/shard_map/front/pallas_call | solution.py:156
  43.0 29.5 %middle.2 = (bf16[8,8,16,1024]{3,2,1,0:T(8,128)(2,1)}, bf16[1024,1024]{1,0:T(8,128)(2,1)}, f32[1024,1024]{1,0:T(8,128)}) custom-call(bf16[8,8,16,1024]{3,2,1,0:T(8,128)(2,1)} %get-tuple-element.35.send_ref, bf16[1024,1024]{1,0:T(8,128)(2,1)} %bitcast.43, bf16[4,2,512,512]{3,2,1,0:T(8,128)(2,1)} %get-tuple-element.37.refs_1_.refs_2_.third_ref.second_ref, ...), custom_call_target="tpu_custom_call" | custom-call | flops 2147483648 | bytes 10485760 | tf_op jit(solution)/shard_map/middle/pallas_call | solution.py:156
  72.5 29.1 %middle.3 = (bf16[8,8,16,1024]{3,2,1,0:T(8,128)(2,1)}, bf16[1024,1024]{1,0:T(8,128)(2,1)}) custom-call(bf16[8,8,16,1024]{3,2,1,0:T(8,128)(2,1)} %bitcast.45, bf16[1024,1024]{1,0:T(8,128)(2,1)} %bitcast.44, bf16[4,2,512,512]{3,2,1,0:T(8,128)(2,1)} %get-tuple-element.37.refs_1_.refs_2_.third_ref.second_ref, ...), custom_call_target="tpu_custom_call" | custom-call | flops 2147483648 | bytes 10485760 | tf_op jit(solution)/shard_map/middle/pallas_call | solution.py:156
  101.6 31.4 %turn.1 = (bf16[8,8,16,1024]{3,2,1,0:T(8,128)(2,1)}, bf16[8,8,16,1024]{3,2,1,0:T(8,128)(2,1)}, bf16[1024,1024]{1,0:T(8,128)(2,1)}, bf16[1024,1024]{1,0:T(8,128)(...) custom-call(bf16[8,8,16,1024]{3,2,1,0:T(8,128)(2,1)} %bitcast.59, ...), custom_call_target="tpu_custom_call" | custom-call | flops 8589934592 | bytes 31457280 | tf_op jit(solution)/shard_map/turn/pallas_call | solution.py:156
  133.1 31.5 %tail.1 = (bf16[8,8,16,1024]{3,2,1,0:T(8,128)(2,1)}, bf16[1024,1024]{1,0:T(8,128)(2,1)}, bf16[1024,1792]{1,0:T(8,128)(2,1)}) custom-call(bf16[8,8,16,1024]{3,2,1,0:T(8,128)(2,1)} %get-tuple-element.42.send_ref, bf16[1024,1024]{1,0:T(8,128)(2,1)} %bitcast.32, bf16[8,8,16,1024]{3,2,1,0:T(8,128)(2,1)} %get-tuple-element.43.refs_1_, ...), custom_call_target="tpu_custom_call" | custom-call | flops 4294967296 | bytes 8388608 | tf_op jit(solution)/shard_map/tail/pallas_call | solution.py:156
  164.6 7.7 %middle_back.1 = (bf16[1024,1024]{1,0:T(8,128)(2,1)}, bf16[1024,1024]{1,0:T(8,128)(2,1)}) custom-call(bf16[1024,1024]{1,0:T(8,128)(2,1)} %bitcast.47, bf16[4,2,512,512]{3,2,1,0:T(8,128)(2,1)} %get-tuple-element.37.refs_1_.refs_2_.third_ref.second_ref, bf16[4,2,512,512]{3,2,1,0:T(8,128)(2,1)} %get-tuple-element.37.refs_1_.refs_2_.third_ref.second_ref, ...), custom_call_target="tpu_custom_call" | custom-call | flops 2147483648 | bytes 12582912 | tf_op jit(solution)/shard_map/middle_back/pallas_call | solution.py:46
  172.3 0.0 reduce-scatter.2.cloned.1.call-update
  172.4 3.6 %collective-permute-start = (bf16[1024,1024]{1,0:T(8,128)(2,1)}, bf16[1024,1024]{1,0:T(8,128)(2,1)S(1)}, u32[]{:S(2)}, u32[]{:S(2)}) collective-permute-start(bf16[1024,1024]{1,0:T(8,128)(2,1)} %get-tuple-element.50), channel_id=1, source_target_pairs={{0,8},{8,16},{16,24},{1,9},{9,17},{17,25},{2,10},{10,18},{18,26},{... | collective-permute-start | bytes 6291464 | tf_op jit(solution)/shard_map/ppermute | solution.py:857
  176.0 58.0 %finish.1 = bf16[8,128,1024]{2,1,0:T(8,128)(2,1)} custom-call(bf16[8,8,16,1024]{3,2,1,0:T(8,128)(2,1)} %bitcast.42, bf16[1024,1024]{1,0:T(8,128)(2,1)} %bitcast.30, bf16[8,128,128]{2,1,0:T(8,128)(2,1)} %bitcast.36, f32[1,1024]{1,0:T(1,128)} %gain_ref.3, bf16[1024,256]{1,0:T(8,128)(2,1)} %bitcast.39, bf16[1024,1024]{1,0:T(8,128)(2,1)} %get-tuple-element.45.refs_10_.dgate_ref, ...), custom_call_target="tpu_custom_call" | custom-call | flops 805306368 | bytes 10485760 | tf_op jit(solution)/shard_map/finish/pallas_call | solution.py:792
  234.0 0.0 collective-permute-done
  234.0 0.0 reduce-scatter.2.cloned.1.call-done.total
  234.1 1.8 split_grads.1
  235.9 0.0 copy-start
  235.9 1.3 copy.23
  237.2 1.0 copy-done
  238.2 1.3 copy.24
Async XLA Ops:
  7.2 226.9 %reduce-scatter.2.cloned.1.call-start = ((), (), s32[]{:S(2)}) async-start(), calls=%async_computation.1 | async-start | bytes 4128768 | tf_op jit(solution)/shard_map/reduce_scatter | solution.py:937
  172.4 61.7 %collective-permute-start = (bf16[1024,1024]{1,0:T(8,128)(2,1)}, bf16[1024,1024]{1,0:T(8,128)(2,1)S(1)}, u32[]{:S(2)}, u32[]{:S(2)}) collective-permute-start(bf16[1024,1024]{1,0:T(8,128)(2,1)} %get-tuple-element.50), channel_id=1, source_target_pairs={{0,8},{8,16},{16,24},{1,9},{9,17},{17,25},{2,10},{10,18},{18,26},{... | collective-permute-start | bytes 6291464 | tf_op jit(solution)/shard_map/ppermute | solution.py:857
  235.9 2.3 copy-start
Sparse Core Ops, SparseCore 0:
  172.5 58.4 reduce-scatter.1
